TPU v7x, 32 devices: a whole 2x2x4 slice. The times are simulated.
32 devices in a mesh: ctx: 8 (over y, x, core), head: 4 (over z).
Axes of the slice: x: 2, y: 2, z: 4, core: 2. Of those that a mesh axis runs over, the one named last changes fastest.
Arguments:
- query_rows: bfloat16 [4096, 2048], P('ctx', 'head'), may hold values from -12 to 12
- key_rows: bfloat16 [4096, 2048], P('ctx', 'head'), may hold values from -12 to 12
- value_rows: bfloat16 [4096, 2048], P('ctx', 'head'), may hold values from -6 to 6
- grad_out: bfloat16 [4096, 2048], P('ctx', 'head'), may hold values from -6 to 6
- house_dirs: float32 [32, 2048], P('ctx', 'head'), may hold values from -6 to 6
- owners: int32 [32, 2], P('ctx'), may hold values from 0 to 7, all different within a row; in each aligned block of 4 rows (0 to 3, 4 to 7, ...) at most 2 rows name the same one
- offsets: int32 [32, 2], P('ctx'), may hold values from 0 to 3
- w_query: bfloat16 [4096, 2048], P(None, 'head'), may hold values from -0.09375 to 0.09375
- w_key: bfloat16 [4096, 2048], P(None, 'head'), may hold values from -0.09375 to 0.09375
- w_value: bfloat16 [4096, 2048], P(None, 'head'), may hold values from -0.09375 to 0.09375
Outputs:
- input_grad: bfloat16 [4096, 4096], P('ctx', 'head')
- house_grad: float32 [32, 2048], P('ctx', 'head')
Inputs may be any that keep to these rules, and one draw needn't show every extreme that they name: `owners`: each query block names 2 different ctx indices; the query blocks of one ctx index name any one ctx index at most 2 times, and exactly 2 times for some.
All inputs are finite; a program needn't handle non-finite values.
Results may differ from a plain program's by a relative error of at most 0.025.
Values may be sent and summed in bfloat16 or wider, within the bound.
No kernel may reach another device: no remote copies, remote signals or barrier semaphores. Data moves between devices by JAX's collectives and lax.ppermute only.
A program may use at most 128 MiB of HBM per device.

v0:
```python
import jax
import jax.numpy as jnp
from jax import lax
from jax.sharding import PartitionSpec as P

DH = 128
BLK = 128
MAXL = 2
CAP = 2


HIGH = lax.Precision.HIGHEST


def prefix_2(value, axis, join, neutral, backward):
    count, mine = (lax.axis_size(axis), lax.axis_index(axis))
    pieces = jax.tree.map(lambda part: lax.all_gather(part, axis), value)
    if backward:
        pieces = jax.tree.map(lambda part: part[::-1], pieces)
        mine = count - 1 - mine
    running = jax.tree.map(
        lambda part, zero: jnp.full_like(part, 0) + jnp.asarray(zero, part.dtype), value, neutral
    )

    def lap(position, running):
        longer = join(running, jax.tree.map(lambda part: part[position], pieces))
        return jax.tree.map(lambda new, old: jnp.where(position < mine, new, old), longer, running)

    return lax.fori_loop(0, count - 1, lap, running)


def reflect_apply(unit_dirs, matrices):
    projected = jnp.einsum("hn,hnk->hk", unit_dirs, matrices, precision=HIGH)
    return matrices - 2.0 * unit_dirs[:, :, None] * projected[:, None, :]


def compose(earlier, latter):
    return jnp.einsum("hmn,hnk->hmk", latter, earlier, precision=HIGH)


def chain_maps(earlier, latter):
    matrix_part = jnp.einsum("hmn,hnk->hmk", latter[0], earlier[0], precision=HIGH)
    offset_part = jnp.einsum("hmn,hnk->hmk", latter[0], earlier[1], precision=HIGH) + latter[1]
    return (matrix_part, offset_part)


def owner_ranks(owner_lists, before):
    same_owner = owner_lists[..., :, None] == owner_lists[..., None, :]
    return jnp.sum((same_owner & before).astype(jnp.int32), axis=-1)


def shards(
    query_rows, key_rows, value_rows, grad_out, house_dirs, owners, offsets, w_query, w_key, w_value
):
    tok_rows, row_width = query_rows.shape
    head_count = row_width // DH
    block_count = tok_rows // BLK
    entries = block_count * MAXL
    ctx_count = lax.axis_size("ctx")
    my_index = lax.axis_index("ctx")
    scaling = DH ** (-0.5)
    house_heads = house_dirs.reshape(block_count, head_count, DH)
    lengths = jnp.sqrt(jnp.sum(house_heads * house_heads, axis=-1, keepdims=True) + 1e-06)
    unit_dirs = house_heads / lengths
    identity = jnp.broadcast_to(jnp.eye(DH, dtype=jnp.float32), (head_count, DH, DH))
    zero_mats = jnp.zeros((head_count, DH, DH), jnp.float32)

    def forward(carry, unit_now):
        updated = reflect_apply(unit_now, carry)
        return (updated, updated)

    local_total, partial_cums = lax.scan(forward, identity, unit_dirs)
    prefix = prefix_2(local_total, "ctx", compose, identity, False)
    cumulative = jnp.einsum("bhmn,hnk->bhmk", partial_cums, prefix, precision=HIGH)
    query_f32 = query_rows.astype(jnp.float32).reshape(block_count, BLK, head_count, DH)
    key_f32 = key_rows.astype(jnp.float32).reshape(block_count, BLK, head_count, DH)
    query_rot = jnp.einsum("bthn,bhnm->bthm", query_f32, cumulative, precision=HIGH).astype(
        jnp.bfloat16
    )
    key_rot = jnp.einsum("bthn,bhnm->bthm", key_f32, cumulative, precision=HIGH).astype(
        jnp.bfloat16
    )
    all_owner, all_offset = (
        lax.all_gather(owners, "ctx", axis=0, tiled=True),
        lax.all_gather(offsets, "ctx", axis=0, tiled=True),
    )
    all_owner = all_owner.reshape(ctx_count, entries)
    all_offset = all_offset.reshape(ctx_count, entries)
    entry_order = jnp.arange(entries)
    before = entry_order[None, :] < entry_order[:, None]
    own_flat = owners.reshape(entries)
    slot_ids = own_flat * CAP + owner_ranks(own_flat, before)
    all_rank = owner_ranks(all_owner, before)
    matched = (all_owner[:, :, None] == my_index) & (
        all_rank[:, :, None] == jnp.arange(CAP)[None, None, :]
    )
    wanted = jnp.sum(jnp.where(matched, all_offset[:, :, None], 0), axis=1).reshape(ctx_count * CAP)
    live_slots = jnp.any(matched, axis=1).reshape(ctx_count * CAP)
    key_flat = key_rot.reshape(block_count, BLK, row_width)
    value_flat = value_rows.reshape(block_count, BLK, row_width)
    sent_keys = key_flat[wanted]
    sent_values = value_flat[wanted]
    got_keys, got_values = (
        lax.all_to_all(sent_keys, "ctx", split_axis=0, concat_axis=0, tiled=True),
        lax.all_to_all(sent_values, "ctx", split_axis=0, concat_axis=0, tiled=True),
    )
    remote_keys = got_keys[slot_ids].reshape(block_count, MAXL * BLK, head_count, DH)
    remote_values = got_values[slot_ids].reshape(block_count, MAXL * BLK, head_count, DH)
    query_tok = query_rot.reshape(tok_rows, head_count, DH)
    key_tok = key_rot.reshape(tok_rows, head_count, DH)
    value_tok = value_rows.reshape(tok_rows, head_count, DH)
    grad_tok = grad_out.reshape(tok_rows, head_count, DH)
    grad_blk = grad_out.reshape(block_count, BLK, head_count, DH)
    position = jnp.arange(tok_rows)
    local_scores = (
        jnp.einsum("thd,uhd->htu", query_tok, key_tok, preferred_element_type=jnp.float32) * scaling
    )
    local_scores = jnp.where(position[:, None] >= position[None, :], local_scores, -jnp.inf)
    remote_scores = (
        jnp.einsum("bthd,bkhd->bhtk", query_rot, remote_keys, preferred_element_type=jnp.float32)
        * scaling
    )

    def to_heads(per_block):
        return per_block.transpose(1, 0, 2).reshape(head_count, tok_rows)

    def to_blocks(per_head):
        return per_head.reshape(head_count, block_count, BLK).transpose(1, 0, 2)

    top_score = jnp.maximum(jnp.max(local_scores, axis=2), to_heads(jnp.max(remote_scores, axis=3)))
    exp_total = jnp.sum(jnp.exp(local_scores - top_score[:, :, None]), axis=2)
    exp_total = exp_total + to_heads(
        jnp.sum(jnp.exp(remote_scores - to_blocks(top_score)[..., None]), axis=3)
    )
    log_total = top_score + jnp.log(exp_total)
    log_blocks = to_blocks(log_total)
    local_probs = jnp.exp(local_scores - log_total[:, :, None])
    remote_probs = jnp.exp(remote_scores - log_blocks[..., None])
    local_pb = local_probs.astype(jnp.bfloat16)
    remote_pb = remote_probs.astype(jnp.bfloat16)
    attended = jnp.einsum("htu,uhd->thd", local_pb, value_tok, preferred_element_type=jnp.float32)
    attended = attended + jnp.einsum(
        "bhtk,bkhd->bthd", remote_pb, remote_values, preferred_element_type=jnp.float32
    ).reshape(tok_rows, head_count, DH)
    delta = jnp.sum(grad_tok.astype(jnp.float32) * attended, axis=2).T
    delta_blocks = to_blocks(delta)
    local_dp = jnp.einsum("thd,uhd->htu", grad_tok, value_tok, preferred_element_type=jnp.float32)
    local_ds = (local_probs * (local_dp - delta[:, :, None])).astype(jnp.bfloat16)
    remote_dp = jnp.einsum(
        "bthd,bkhd->bhtk", grad_blk, remote_values, preferred_element_type=jnp.float32
    )
    remote_ds = (remote_probs * (remote_dp - delta_blocks[..., None])).astype(jnp.bfloat16)
    dq_rot = jnp.einsum("htu,uhd->thd", local_ds, key_tok, preferred_element_type=jnp.float32)
    dq_rot = scaling * (
        dq_rot
        + jnp.einsum(
            "bhtk,bkhd->bthd", remote_ds, remote_keys, preferred_element_type=jnp.float32
        ).reshape(tok_rows, head_count, DH)
    )
    dk_local = scaling * jnp.einsum(
        "htu,thd->uhd", local_ds, query_tok, preferred_element_type=jnp.float32
    )
    dv_local = jnp.einsum("htu,thd->uhd", local_pb, grad_tok, preferred_element_type=jnp.float32)
    slot_count = ctx_count * CAP
    empty_slots = jnp.zeros((slot_count, BLK, row_width), jnp.bfloat16)
    part_key = (
        scaling
        * jnp.einsum("bhtk,bthd->bkhd", remote_ds, query_rot, preferred_element_type=jnp.float32)
    ).astype(jnp.bfloat16)
    part_value = jnp.einsum(
        "bhtk,bthd->bkhd", remote_pb, grad_blk, preferred_element_type=jnp.float32
    ).astype(jnp.bfloat16)
    back_keys, back_values = (
        lax.all_to_all(
            empty_slots.at[slot_ids].set(part_key.reshape(entries, BLK, row_width)),
            "ctx",
            split_axis=0,
            concat_axis=0,
            tiled=True,
        ),
        lax.all_to_all(
            empty_slots.at[slot_ids].set(part_value.reshape(entries, BLK, row_width)),
            "ctx",
            split_axis=0,
            concat_axis=0,
            tiled=True,
        ),
    )
    pick_table = (
        (wanted[None, :] == jnp.arange(block_count)[:, None]) & live_slots[None, :]
    ).astype(jnp.bfloat16)
    dk_rot = dk_local.reshape(block_count, BLK, head_count, DH)
    dk_rot = dk_rot + jnp.einsum(
        "bs,srw->brw", pick_table, back_keys, preferred_element_type=jnp.float32
    ).reshape(block_count, BLK, head_count, DH)
    dv_all = dv_local.reshape(block_count, BLK, head_count, DH)
    dv_all = dv_all + jnp.einsum(
        "bs,srw->brw", pick_table, back_values, preferred_element_type=jnp.float32
    ).reshape(block_count, BLK, head_count, DH)
    dq_rot = dq_rot.reshape(block_count, BLK, head_count, DH)
    dq_out = (
        jnp.einsum("bthm,bhnm->bthn", dq_rot, cumulative, precision=HIGH)
        .astype(jnp.bfloat16)
        .reshape(tok_rows, row_width)
    )
    dk_out = (
        jnp.einsum("bthm,bhnm->bthn", dk_rot, cumulative, precision=HIGH)
        .astype(jnp.bfloat16)
        .reshape(tok_rows, row_width)
    )
    dv_out = dv_all.astype(jnp.bfloat16).reshape(tok_rows, row_width)
    dcum = jnp.einsum("bthn,bthm->bhnm", query_f32, dq_rot, precision=HIGH)
    dcum = dcum + jnp.einsum("bthn,bthm->bhnm", key_f32, dk_rot, precision=HIGH)

    def backward(carry, inputs):
        dcum_now, unit_now = inputs
        adjoint = dcum_now + carry
        return (reflect_apply(unit_now, adjoint), adjoint)

    outgoing, _ = lax.scan(backward, zero_mats, (dcum, unit_dirs), reverse=True)
    _, incoming = prefix_2(
        (jnp.swapaxes(local_total, 1, 2), outgoing), "ctx", chain_maps, (identity, zero_mats), True
    )
    _, adjoints = lax.scan(backward, incoming, (dcum, unit_dirs), reverse=True)
    previous = jnp.concatenate([prefix[None], cumulative[:-1]], axis=0)
    dreflect = jnp.einsum("bhmn,bhkn->bhmk", adjoints, previous, precision=HIGH)
    dunit = jnp.einsum("bhmn,bhn->bhm", dreflect, unit_dirs, precision=HIGH)
    dunit = -2.0 * (dunit + jnp.einsum("bhnm,bhn->bhm", dreflect, unit_dirs, precision=HIGH))
    house_grad = (dunit - unit_dirs * jnp.sum(unit_dirs * dunit, axis=-1, keepdims=True)) / lengths
    house_grad = house_grad.reshape(block_count, row_width)
    summed = jnp.zeros(
        (w_query.shape[0] // lax.axis_size("head") * lax.axis_size("head"), tok_rows), jnp.float32
    )
    for weight_mat, grad_mat in ((w_query, dq_out), (w_key, dk_out), (w_value, dv_out)):
        summed = summed + lax.dot_general(
            weight_mat, grad_mat, (((1,), (1,)), ((), ())), preferred_element_type=jnp.float32
        )
    share = lax.psum_scatter(
        summed.astype(jnp.bfloat16), "head", scatter_dimension=0, tiled=True
    ).astype(jnp.float32)
    return (share.T.astype(jnp.bfloat16), house_grad)


def solution(mesh):
    placed = (
        P("ctx", "head"),
        P("ctx", "head"),
        P("ctx", "head"),
        P("ctx", "head"),
        P("ctx", "head"),
        P("ctx", None),
        P("ctx", None),
        P(None, "head"),
        P(None, "head"),
        P(None, "head"),
    )
    return jax.shard_map(
        shards,
        mesh=mesh,
        in_specs=placed,
        out_specs=(P("ctx", "head"), P("ctx", "head")),
        check_vma=False,
    )
```

profile of v0, /device:TPU:0, one launch (start us, length us, event | category | flops | bytes accessed | tf_op | source)
XLA Modules:
  0.0 309.6 jit_solution(4069486764182931905)
XLA Ops:
  11.1 10.3 %all-gather.3 = s32[8,4,2]{1,2,0:T(2,128)S(1)} all-gather(s32[1,4,2]{1,2,0:T(2,128)S(1)} %bitcast.316), channel_id=1, replica_groups=mesh['ctx'=8,'head'=4] {'ctx'}, dimensions={0}, use_global_device_ids=true | all-gather | bytes 288 | tf_op jit(solution)/shard_map/all_gather | solution.py:84
  21.7 8.9 %all-gather.4 = s32[8,4,2]{1,2,0:T(2,128)S(1)} all-gather(s32[1,4,2]{1,2,0:T(2,128)S(1)} %bitcast.320), channel_id=1, replica_groups=mesh['ctx'=8,'head'=4] {'ctx'}, dimensions={0}, use_global_device_ids=true | all-gather | bytes 288 | tf_op jit(solution)/shard_map/all_gather | solution.py:85
  33.4 4.5 %all-to-all-start.1 = ((bf16[16,128,512]{2,1,0:T(8,128)(2,1)}), bf16[16,128,512]{2,1,0:T(8,128)(2,1)}, u32[]{:S(2)}, u32[]{:S(2)}) async-start(bf16[16,128,512]{2,1,0:T(8,128)(2,1)} %gather_fusion.2), calls=%async_computation.1 | async-start | bytes 4194304 | tf_op jit(solution)/shard_map/all_to_all | solution.py:105
  38.0 3.8 %all-gather.9.cloned.1.call-done = f32[32,128,128]{2,1,0:T(8,128)} async-done(((f32[4,128,128]{2,1,0:T(8,128)}), f32[32,128,128]{2,1,0:T(8,128)}) %all-gather.9.cloned.1.call-update) | async-done | bytes 2097168 | tf_op jit(solution)/shard_map/all_gather | solution.py:17
  41.8 9.8 %while.71 = (s32[]{:T(128)}, f32[4,128,128]{2,1,0:T(8,128)S(1)}, s32[]{:T(128)}, f32[8,4,128,128]{3,2,1,0:T(8,128)}, s32[]{:T(128)}) while((s32[]{:T(128)}, f32[4,128,128]{2,1,0:T(8,128)S(1)}, s32[]{:T(128)}, f32[8,4,128,128]{3,2,1,0:T(8,128)}, s32[]{:T(128)}) %tuple.187), condition=%wide.region_4.5_spmd, body=%wide.region_3.4_spmd.sunk | while | flops 100728832 | bytes 1573447 | solution.py:29
  56.3 8.2 %all-to-all-done.1 = bf16[16,128,512]{2,1,0:T(8,128)(2,1)} async-done(((bf16[16,128,512]{2,1,0:T(8,128)(2,1)}), bf16[16,128,512]{2,1,0:T(8,128)(2,1)}, u32[]{:S(2)}, u32[]{:S(2)}) %all-to-all-start.1) | async-done | bytes 2097184 | tf_op jit(solution)/shard_map/all_to_all | solution.py:105
  64.5 4.4 %all-to-all-start = ((bf16[16,128,512]{2,1,0:T(8,128)(2,1)}), bf16[16,128,512]{2,1,0:T(8,128)(2,1)}, u32[]{:S(2)}, u32[]{:S(2)}) async-start(bf16[16,128,512]{2,1,0:T(8,128)(2,1)} %gather_fusion), calls=%async_computation | async-start | bytes 4194304 | tf_op jit(solution)/shard_map/all_to_all | solution.py:104
  74.1 3.3 %gather_fusion.3 = bf16[8,128,512]{2,1,0:T(8,128)(2,1)} fusion(bf16[16,128,512]{2,1,0:T(8,128)(2,1)} %all-to-all-done.1, s32[1024]{0:T(1024)S(1)} %pad_clamp_fusion), kind=kCustom, calls=%fused_computation.3 | custom fusion | bytes 2097184 | tf_op jit(solution)/shard_map/gather | solution.py:108
  84.8 13.5 %all-to-all-done = bf16[16,128,512]{2,1,0:T(8,128)(2,1)} async-done(((bf16[16,128,512]{2,1,0:T(8,128)(2,1)}), bf16[16,128,512]{2,1,0:T(8,128)(2,1)}, u32[]{:S(2)}, u32[]{:S(2)}) %all-to-all-start) | async-done | bytes 2097184 | tf_op jit(solution)/shard_map/all_to_all | solution.py:104
  112.6 4.3 %fusion.33 = f32[512,4]{0,1:T(4,128)S(1)} fusion(f32[512,4,128]{0,2,1:T(8,128)} %reshape.265, bf16[512,4,128]{0,2,1:T(8,128)(2,1)} %bitcast.303, bf16[512,4,128]{0,2,1:T(8,128)(2,1)} %bitcast.300, f32[4,512,512]{1,2,0:T(8,128)} %get-tuple-element.533, f32[4,512]{1,0:T(4,128)S(1)} %fusion.75, pred[512,512]{0,1:T(8,128)(4,1)} %copy-done.28), kind=kOutput, calls=%fused_computation.76 | convolution fusion | flops 273676288 | bytes 6569984 | tf_op jit(solution)/shard_map/htu,uhd->thd/dot_general | solution.py:141
  126.5 3.3 %scatter_fusion = bf16[16,128,512]{2,1,0:T(8,128)(2,1)} fusion(bf16[16,128,512]{2,1,0:T(8,128)(2,1)} %broadcast_in_dim.89.clone.1, s32[8]{0:T(128)S(1)} %fusion.86, bf16[8,128,512]{2,1,0:T(8,128)(2,1)} %reshape.315), kind=kCustom, calls=%fused_computation.4 | custom fusion | bytes 3145760 | tf_op jit(solution)/shard_map/scatter | solution.py:175
  129.8 4.6 %all-to-all-start.2 = ((bf16[16,128,512]{2,1,0:T(8,128)(2,1)}), bf16[16,128,512]{2,1,0:T(8,128)(2,1)}, u32[]{:S(2)}, u32[]{:S(2)}) async-start(bf16[16,128,512]{2,1,0:T(8,128)(2,1)} %scatter_fusion), calls=%async_computation.2 | async-start | bytes 4194304 | tf_op jit(solution)/shard_map/all_to_all | solution.py:174
  150.2 4.0 %multiply_convert_fusion = bf16[4,512,512]{1,2,0:T(8,128)(2,1)S(1)} fusion(f32[4,512,512]{1,2,0:T(8,128)} %get-tuple-element.533, bf16[512,4,128]{0,2,1:T(8,128)(2,1)} %bitcast.304, bf16[512,4,128]{0,2,1:T(8,128)(2,1)S(1)} %bitcast.302, f32[4,512]{1,0:T(4,128)S(1)} %bitcast.323, f32[4,512]{1,0:T(4,128)S(1)} %fusion.75, pred[512,512]{0,1:T(8,128)(4,1)S(1)} %copy-done.30), kind=kOutput, calls=%fused_computation.38 | convolution fusion | flops 274726912 | bytes 7618560 | tf_op jit(solution)/shard_map/thd,uhd->htu/dot_general | solution.py:147
  161.0 4.4 %all-to-all-start.3 = ((bf16[16,128,512]{2,1,0:T(8,128)(2,1)}), bf16[16,128,512]{2,1,0:T(8,128)(2,1)}, u32[]{:S(2)}, u32[]{:S(2)}) async-start(bf16[16,128,512]{2,1,0:T(8,128)(2,1)} %scatter_fusion.1), calls=%async_computation.3 | async-start | bytes 4194304 | tf_op jit(solution)/shard_map/all_to_all | solution.py:181
  165.4 3.9 %fusion.21 = f32[4,128,512]{2,0,1:T(4,128)} fusion(bf16[16,128,512]{2,1,0:T(8,128)(2,1)} %all-to-all-done.2, s32[16]{0:T(128)S(1)} %eq.85, pred[16]{0:T(512)(128)(4,1)S(1)} %and.35), kind=kOutput, calls=%fused_computation.48 | convolution fusion | flops 8388736 | bytes 3145808 | tf_op jit(solution)/shard_map/bs,srw->brw/dot_general | solution.py:193
  179.9 3.9 %fusion.34 = bf16[4,128,4,128]{1,3,2,0:T(8,128)(2,1)} fusion(f32[4,16,4,8,128]{4,3,2,1,0:T(8,128)} %copy-done.12, f32[4,4,128,128]{2,3,0,1:T(8,128)S(1)} %convolution_bitcast_fusion.4), kind=kOutput, calls=%fused_computation.77 | convolution fusion | flops 402915328 | bytes 2621440 | tf_op jit(solution)/shard_map/bthm,bhnm->bthn/dot_general | solution.py:202
  185.1 4.5 %fusion.92 = f32[4,512,128]{1,2,0:T(8,128)} fusion(bf16[512,4,128]{0,2,1:T(8,128)(2,1)} %bitcast.301, f32[4,512,512]{1,2,0:T(8,128)} %get-tuple-element.533, f32[4,512]{1,0:T(4,128)S(1)} %fusion.75, pred[512,512]{0,1:T(8,128)(4,1)S(1)} %copy-done.31), kind=kOutput, calls=%fused_computation.159 | convolution fusion | flops 272629760 | bytes 6037504 | tf_op jit(solution)/shard_map/htu,thd->uhd/dot_general | solution.py:163
  192.2 8.0 %fusion.61 = f32[512,4096]{1,0:T(8,128)} fusion(bf16[4096,512]{1,0:T(8,128)(2,1)} %param.27, bf16[64,8,4,128]{3,2,1,0:T(4,128)(2,1)S(1)} %bitcast.293), kind=kOutput, calls=%fused_computation.108 | convolution fusion | flops 2147483648 | bytes 13107200 | tf_op jit(solution)/shard_map/dot_general | solution.py:235
  209.5 5.6 %fusion.58 = f32[512,4096]{1,0:T(8,128)} fusion(bf16[4096,512]{1,0:T(8,128)(2,1)S(1)} %copy-done.22, bf16[64,8,4,128]{3,2,1,0:T(4,128)(2,1)S(1)} %bitcast.292), kind=kOutput, calls=%fused_computation.105 | convolution fusion | flops 2147483648 | bytes 13107200 | tf_op jit(solution)/shard_map/dot_general | solution.py:235
  215.1 9.2 %fusion.15 = bf16[4096,512]{0,1:T(8,128)(2,1)} fusion(bf16[512,512]{1,0:T(8,128)(2,1)S(1)} %fusion.46, bf16[4096,512]{1,0:T(8,128)(2,1)} %param.29, f32[512,4096]{1,0:T(8,128)S(1)} %bitcast.282, f32[512,4096]{1,0:T(8,128)} %fusion.58), kind=kOutput, calls=%fused_computation.37 | convolution fusion | flops 2153775104 | bytes 25690112 | tf_op jit(solution)/shard_map/dot_general | solution.py:235
  228.6 3.2 %rev.7 = f32[8,4,128,128]{3,2,1,0:T(8,128)} reverse(f32[8,4,128,128]{3,2,1,0:T(8,128)} %bitcast.295), dimensions={0} | reverse | bytes 4194304 | tf_op jit(solution)/shard_map/rev | solution.py:19
  231.8 10.5 %while.74 = (s32[]{:T(128)}, f32[4,128,128]{2,1,0:T(8,128)S(1)}, s32[]{:T(128)}, f32[8,4,128,128]{3,2,1,0:T(8,128)}, f32[8,4,128,128]{3,2,1,0:T(8,128)}, /*index=5*/s32[]{:T(128)}, s32[]{:T(128)}) while((s32[]{:T(128)}, f32[4,128,128]{2,1,0:T(8,128)S(1)}, s32[]{:T(128)}, f32[8,4,128,128]{3,2,1,0:T(8,128)}, ...), condition=%wide.region_20.21_spmd.clone, body=%wide.region_19.20_spmd.clone.sunk | while | flops 100925440 | bytes 1837663 | solution.py:29
  243.5 4.9 %while.72 = (s32[]{:T(128)}, f32[4,128,128]{2,1,0:T(8,128)S(1)}, f32[4,4,128,128]{3,2,1,0:T(8,128)}, f32[4,4,128,128]{3,2,1,0:T(8,128)S(1)}, f32[4,4,128]{2,1,0:T(4,128)S(1)}, /*index=5*/s32[]{:T(128)}, s32[]{:T(128)}) while((s32[]{:T(128)}, f32[4,128,128]{2,1,0:T(8,128)S(1)}, f32[4,4,128,128]{3,2,1,0:T(8,128)}, ...), condition=%wide.region_22.23_spmd, body=%wide.region_21.22_spmd.sunk | while | flops 983555 | bytes 1849441 | solution.py:224
  254.3 48.5 %reduce-scatter.2.cloned.1.call-done = bf16[1024,512]{0,1:T(8,128)(2,1)} async-done(((bf16[4096,512]{0,1:T(8,128)(2,1)}), bf16[1024,512]{0,1:T(8,128)(2,1)}) %reduce-scatter.2.cloned.1.call-update) | async-done | bytes 1048592 | tf_op jit(solution)/shard_map/reduce_scatter | solution.py:238
  (265 shorter events, 134.2 us)
Async XLA Ops:
  7.2 34.7 %all-gather.9.cloned.1.call-start = ((), (), s32[]{:S(2)}) async-start(), calls=%async_computation.6 | async-start | bytes 2359296 | tf_op jit(solution)/shard_map/all_gather | solution.py:17
  8.2 13.5 %copy-start.38 = (s32[4,2]{0,1:T(2,128)S(1)}, s32[4,2]{0,1:T(2,128)}, u32[]{:S(2)}) copy-start(s32[4,2]{0,1:T(2,128)} %param.26) | copy-start | bytes 100
  8.2 23.2 %copy-start.7 = (bf16[512,512]{1,0:T(8,128)(2,1)S(1)}, bf16[512,512]{1,0:T(8,128)(2,1)}, u32[]{:S(2)}) copy-start(bf16[512,512]{1,0:T(8,128)(2,1)} %param.22) | copy-start | bytes 1572868
  33.4 31.1 %all-to-all-start.1 = ((bf16[16,128,512]{2,1,0:T(8,128)(2,1)}), bf16[16,128,512]{2,1,0:T(8,128)(2,1)}, u32[]{:S(2)}, u32[]{:S(2)}) async-start(bf16[16,128,512]{2,1,0:T(8,128)(2,1)} %gather_fusion.2), calls=%async_computation.1 | async-start | bytes 4194304 | tf_op jit(solution)/shard_map/all_to_all | solution.py:105
  38.0 14.8 %copy-start.15 = (bf16[4,128,4,128]{3,2,1,0:T(4,128)(2,1)}, bf16[4,128,4,128]{3,2,1,0:T(4,128)(2,1)S(1)}, u32[]{:S(2)}) copy-start(bf16[4,128,4,128]{3,2,1,0:T(4,128)(2,1)S(1)} %reshape.252) | copy-start | bytes 1572868
  52.8 171.6 %copy-start.2 = (f32[4,4,128,128]{2,3,0,1:T(8,128)}, f32[4,4,128,128]{2,3,0,1:T(8,128)S(1)}, u32[]{:S(2)}) copy-start(f32[4,4,128,128]{2,3,0,1:T(8,128)S(1)} %convolution_bitcast_fusion.4) | copy-start | bytes 3145732
  56.3 12.8 %copy-start.1 = (f32[4,128,128]{2,1,0:T(8,128)S(1)}, f32[4,128,128]{2,1,0:T(8,128)}, u32[]{:S(2)}) copy-start(f32[4,128,128]{2,1,0:T(8,128)} %copy-done) | copy-start | bytes 786436
  56.3 14.8 %copy-start.33 = (bf16[512,512]{1,0:T(8,128)(2,1)S(1)}, bf16[512,512]{1,0:T(8,128)(2,1)}, u32[]{:S(2)}) copy-start(bf16[512,512]{1,0:T(8,128)(2,1)} %param.23) | copy-start | bytes 1572868
  64.5 33.8 %all-to-all-start = ((bf16[16,128,512]{2,1,0:T(8,128)(2,1)}), bf16[16,128,512]{2,1,0:T(8,128)(2,1)}, u32[]{:S(2)}, u32[]{:S(2)}) async-start(bf16[16,128,512]{2,1,0:T(8,128)(2,1)} %gather_fusion), calls=%async_computation | async-start | bytes 4194304 | tf_op jit(solution)/shard_map/all_to_all | solution.py:104
  68.8 4.5 %copy-start.35 = (bf16[512,512]{1,0:T(8,128)(2,1)S(1)}, bf16[512,512]{1,0:T(8,128)(2,1)}, u32[]{:S(2)}) copy-start(bf16[512,512]{1,0:T(8,128)(2,1)} %param.20) | copy-start | bytes 1572868
  68.9 156.5 %all-gather.11.cloned.1.call-start = ((), (), s32[]{:S(2)}) async-start(), calls=%async_computation.7 | async-start | bytes 2359296 | tf_op jit(solution)/shard_map/all_gather | solution.py:17
  73.5 6.1 %copy-start.16 = (bf16[4,128,4,128]{3,2,1,0:T(4,128)(2,1)}, bf16[4,128,4,128]{3,2,1,0:T(4,128)(2,1)S(1)}, u32[]{:S(2)}) copy-start(bf16[4,128,4,128]{3,2,1,0:T(4,128)(2,1)S(1)} %reshape.254) | copy-start | bytes 1572868
  74.1 7.9 %copy-start.28 = (pred[512,512]{0,1:T(8,128)(4,1)}, pred[512,512]{0,1:T(8,128)(4,1)S(1)}, u32[]{:S(2)}) copy-start(pred[512,512]{0,1:T(8,128)(4,1)S(1)} %iota_compare_fusion) | copy-start | bytes 786436
  129.8 31.2 %all-to-all-start.2 = ((bf16[16,128,512]{2,1,0:T(8,128)(2,1)}), bf16[16,128,512]{2,1,0:T(8,128)(2,1)}, u32[]{:S(2)}, u32[]{:S(2)}) async-start(bf16[16,128,512]{2,1,0:T(8,128)(2,1)} %scatter_fusion), calls=%async_computation.2 | async-start | bytes 4194304 | tf_op jit(solution)/shard_map/all_to_all | solution.py:174
  155.6 15.4 %copy-start.8 = (f32[4,16,4,8,128]{4,3,2,1,0:T(8,128)}, f32[4,16,4,8,128]{4,3,2,1,0:T(8,128)S(1)}, u32[]{:S(2)}) copy-start(f32[4,16,4,8,128]{4,3,2,1,0:T(8,128)S(1)} %fusion.32) | copy-start | bytes 3145732
  161.0 43.2 %all-to-all-start.3 = ((bf16[16,128,512]{2,1,0:T(8,128)(2,1)}), bf16[16,128,512]{2,1,0:T(8,128)(2,1)}, u32[]{:S(2)}, u32[]{:S(2)}) async-start(bf16[16,128,512]{2,1,0:T(8,128)(2,1)} %scatter_fusion.1), calls=%async_computation.3 | async-start | bytes 4194304 | tf_op jit(solution)/shard_map/all_to_all | solution.py:181
  165.4 63.2 %all-gather.13.cloned.1.call-start = ((), (), s32[]{:S(2)}) async-start(), calls=%async_computation.8 | async-start | bytes 2359296 | tf_op jit(solution)/shard_map/all_gather | solution.py:17
  178.7 6.4 %copy-start.31 = (pred[512,512]{0,1:T(8,128)(4,1)S(1)}, pred[512,512]{0,1:T(8,128)(4,1)}, u32[]{:S(2)}) copy-start(pred[512,512]{0,1:T(8,128)(4,1)} %copy-done.28) | copy-start | bytes 786436
  179.4 123.4 %reduce-scatter.2.cloned.1.call-start = ((), (), s32[]{:S(2)}) async-start(), calls=%async_computation.5 | async-start | bytes 5242880 | tf_op jit(solution)/shard_map/reduce_scatter | solution.py:238
  192.2 8.0 %copy-start.9 = (f32[4,16,4,8,128]{4,3,2,1,0:T(8,128)S(1)}, f32[4,16,4,8,128]{4,3,2,1,0:T(8,128)}, u32[]{:S(2)}) copy-start(f32[4,16,4,8,128]{4,3,2,1,0:T(8,128)} %copy-done.8) | copy-start | bytes 3145732
  192.2 8.0 %copy-start.11 = (f32[4,128,512]{1,2,0:T(8,128)S(1)}, f32[4,128,512]{1,2,0:T(8,128)}, u32[]{:S(2)}) copy-start(f32[4,128,512]{1,2,0:T(8,128)} %copy-done.10) | copy-start | bytes 3145732
  207.6 7.5 %slice-start.1 = ((s8[8388608]{0:T(1024)(128)(4,1)}), s8[4194304]{0:T(1024)(128)(4,1)S(1)}, s32[]{:S(2)}) async-start(s8[8388608]{0:T(1024)(128)(4,1)} %bitcast.281), calls=%async_computation.10 | async-start | bytes 8388608
  209.5 5.6 %slice-start.2 = ((s8[8388608]{0:T(1024)(128)(4,1)}), s8[4194304]{0:T(1024)(128)(4,1)S(1)}, s32[]{:S(2)}) async-start(s8[8388608]{0:T(1024)(128)(4,1)} %bitcast.281), calls=%async_computation.11 | async-start | bytes 8388608
  243.5 4.9 %slice-start = ((f32[4,4,128,128]{2,3,0,1:T(8,128)}), f32[3,4,128,128]{2,3,0,1:T(8,128)S(1)}, s32[]{:S(2)}) async-start(f32[4,4,128,128]{2,3,0,1:T(8,128)} %copy-done.2), calls=%async_computation.9 | async-start | bytes 1572864 | tf_op jit(solution)/shard_map/slice | solution.py:225
  (26 other events, 58.5 us)
Sparse Core Ops, SparseCore 0:
  11.2 30.6 all-gather.8
  71.6 37.8 all-gather.10
  179.6 29.4 all-gather.12
  224.4 78.3 reduce-scatter.1
where the time goes:
time: 315 us; the launch traced here: 310 us
  matrix products  101 us (32%)
  waiting for transfers between devices  76.5 us (24%)
  local copies, waits for them, and re-layouts  70.8 us (22%)
  blocking collectives  19.2 us (6%)
  starting transfers between devices  18.5 us (6%)
  between operations  14.7 us (5%)
  other arithmetic  8.21 us (3%)
    reduce_scatter x1, waiting for transfers between devices, shards(): lax.psum_scatter(summed.astype(jnp.bfloat16), 'head', scatter_dimension=0...  48.5 us
    dot_general x3, matrix products, shards(): lax.dot_general(weight_mat, grad_mat, (((1,), (1,)), ((), ())), preferred...  22.8 us
    all_to_all x1, waiting for transfers between devices, shards(): lax.all_to_all(sent_keys, 'ctx', split_axis=0, concat_axis=0, tiled=True)  13.5 us
    unnamed x86, local copies, waits for them, and re-layouts  11.9 us
    all_gather x1, blocking collectives, shards(): lax.all_gather(owners, 'ctx', axis=0, tiled=True)  10.3 us
    dot_general x7, matrix products, chain_maps(): jnp.einsum('hmn,hnk->hmk', latter[0], earlier[1], precision=HIGH)  10.2 us
    dot_general x7, matrix products, compose(): return jnp.einsum('hmn,hnk->hmk', latter, earlier, precision=HIGH)  9.46 us
    all_gather x1, blocking collectives, shards(): lax.all_gather(offsets, 'ctx', axis=0, tiled=True)  8.86 us
  transfers between devices with their start and end apart: 8, of which 5 were waited for; matrix products, arithmetic and copies ran while one was open for 54% of the time, Pallas kernels for 0%

commit v1 on v0

v1 whole, which is shorter than its diff:
```python
import functools

import jax
import jax.numpy as jnp
from jax import lax
from jax.experimental import pallas as pl
from jax.experimental.pallas import tpu as pltpu
from jax.sharding import PartitionSpec as P

DH = 128
BLK = 128
MAXL = 2
HIGH = lax.Precision.HIGHEST
F32 = jnp.float32
BF16 = jnp.bfloat16
VMEM_BYTES = 52 * 1024 * 1024


def nn(a, b):
    return lax.dot_general(a, b, (((1,), (0,)), ((), ())), preferred_element_type=F32)


def nt(a, b):
    return lax.dot_general(a, b, (((1,), (1,)), ((), ())), preferred_element_type=F32)


def tn(a, b):
    return lax.dot_general(a, b, (((0,), (0,)), ((), ())), preferred_element_type=F32)


def nn_high(a, b):
    return lax.dot_general(
        a, b, (((1,), (0,)), ((), ())), precision=HIGH, preferred_element_type=F32
    )


def nt_high(a, b):
    return lax.dot_general(
        a, b, (((1,), (1,)), ((), ())), precision=HIGH, preferred_element_type=F32
    )


def split(value):
    top = value.astype(BF16)
    return top, (value - top.astype(F32)).astype(BF16)


def iota(shape, dim):
    return lax.broadcasted_iota(jnp.int32, shape, dim)


def head(h):
    return slice(h * DH, (h + 1) * DH)


def compiler_params():
    return pltpu.CompilerParams(vmem_limit_bytes=VMEM_BYTES)


def in_vmem(count):
    return [pl.BlockSpec(memory_space=pltpu.VMEM)] * count


def chain_kernel(
    heads,
    blocks,
    base_ref,
    owners_ref,
    offsets_ref,
    house_ref,
    query_ref,
    key_ref,
    unit_ref,
    rows_ref,
    inv_ref,
    qrot_ref,
    krot_ref,
    local_ref,
    list_hi_ref,
    list_lo_ref,
    unit_t,
    unit_h,
):
    count = house_ref.shape[0]
    eye = (iota((count, count), 0) == iota((count, count), 1)).astype(F32)
    for h in range(heads):
        house = house_ref[:, head(h)]
        lengths = jnp.sqrt(jnp.sum(house * house, axis=1, keepdims=True) + 1e-06)
        unit_ref[:, head(h)] = house / lengths
        unit_h[h] = house / lengths
        inv_ref[h] = eye

    def eliminate(step, carry):
        below = iota((count, 1), 0) > step
        for h in range(heads):
            pivot = unit_h[h, pl.ds(step, 1), :]
            overlap = jnp.sum(unit_h[h] * pivot, axis=1, keepdims=True)
            factor = jnp.where(below, 2.0 * overlap, 0.0)
            inv_ref[h] = inv_ref[h] - factor * inv_ref[h, pl.ds(step, 1), :]
        return carry

    lax.fori_loop(0, count, eliminate, 0)
    eye_wide = (iota((DH, DH), 0) == iota((DH, DH), 1)).astype(F32)
    for h in range(heads):
        units = unit_ref[:, head(h)]
        rows_ref[:, head(h)] = nn_high(inv_ref[h], units)
        unit_t[h] = nt_high(eye_wide, units)

    def cumulative(h, block):
        kept = jnp.where(iota((DH, count), 1) <= block, unit_t[h], 0.0)
        return split(eye_wide - 2.0 * nn_high(kept, rows_ref[:, head(h)]))

    base = base_ref[0] * blocks

    def local_block(b, carry):
        here = pl.ds(pl.multiple_of(b * BLK, BLK), BLK)
        for h in range(heads):
            hi, lo = cumulative(h, base + b)
            local_ref[b, h] = hi
            query, key = query_ref[here, head(h)], key_ref[here, head(h)]
            qrot_ref[here, head(h)] = (nn(query, hi) + nn(query, lo)).astype(BF16)
            krot_ref[here, head(h)] = (nn(key, hi) + nn(key, lo)).astype(BF16)
        return carry

    lax.fori_loop(0, blocks, local_block, 0)

    def listed_block(e, carry):
        a, l = e // MAXL, e % MAXL
        block = owners_ref[a, l] * blocks + offsets_ref[a, l]
        for h in range(heads):
            hi, lo = cumulative(h, block)
            list_hi_ref[e, h] = hi
            list_lo_ref[e, h] = lo
        return carry

    lax.fori_loop(0, blocks * MAXL, listed_block, 0)


def run_chain(me, owners, offsets, house_all, query_rows, key_rows, heads, blocks):
    count = house_all.shape[0]
    rows, width = query_rows.shape
    entries = blocks * MAXL
    smem = [pl.BlockSpec(memory_space=pltpu.SMEM)] * 3
    return pl.pallas_call(
        functools.partial(chain_kernel, heads, blocks),
        out_shape=[
            jax.ShapeDtypeStruct((count, width), F32),
            jax.ShapeDtypeStruct((count, width), F32),
            jax.ShapeDtypeStruct((heads, count, count), F32),
            jax.ShapeDtypeStruct((rows, width), BF16),
            jax.ShapeDtypeStruct((rows, width), BF16),
            jax.ShapeDtypeStruct((blocks, heads, DH, DH), BF16),
            jax.ShapeDtypeStruct((entries, heads, DH, DH), BF16),
            jax.ShapeDtypeStruct((entries, heads, DH, DH), BF16),
        ],
        in_specs=smem + in_vmem(3),
        out_specs=in_vmem(8),
        scratch_shapes=[
            pltpu.VMEM((heads, DH, count), F32),
            pltpu.VMEM((heads, count, DH), F32),
        ],
        compiler_params=compiler_params(),
        name="house_chain",
    )(me, owners, offsets, house_all, query_rows, key_rows)


def attend_kernel(heads, blocks, sources, pieces, *refs):
    me_ref, owners_ref, offsets_ref = refs[:3]
    key_srcs = refs[3 : 3 + sources]
    value_srcs = refs[3 + sources : 3 + 2 * sources]
    refs = refs[3 + 2 * sources :]
    (query_ref, qrot_ref, krot_ref, value_ref, grad_ref, local_ref, hi_ref, lo_ref) = refs[:8]
    dq_ref, dcum_ref, dk_ref, dv_ref = refs[8:12]
    outs = refs[12 : 12 + max(pieces, 1)]
    refs = refs[12 + max(pieces, 1) :]
    far_keys, far_values, sems = refs[:3]
    width = heads * DH
    entries = blocks * MAXL
    scaling = DH ** (-0.5)

    def start(e, src, kind, slot, where):
        pltpu.make_async_copy(src.at[where], slot.at[e], sems.at[kind, e]).start()

    for e in range(entries):
        owner, offset = owners_ref[e // MAXL, e % MAXL], offsets_ref[e // MAXL, e % MAXL]
        here = pl.ds(pl.multiple_of(offset * BLK, BLK), BLK)
        if sources == 1:
            start(e, key_srcs[0], 0, far_keys, (owner, here))
            start(e, value_srcs[0], 1, far_values, (owner, here))
        else:
            distance = owner ^ me_ref[0]
            for r in range(sources):

                @pl.when(distance == r)
                def _():
                    start(e, key_srcs[r], 0, far_keys, here)
                    start(e, value_srcs[r], 1, far_values, here)

    if pieces:
        payload, out_sems = refs[3:5]
        payload[...] = jnp.zeros_like(payload)
    else:
        payload = None
    for kind, slots in ((0, far_keys), (1, far_values)):
        for e in range(entries):
            pltpu.make_async_copy(slots.at[e], slots.at[e], sems.at[kind, e]).wait()

    for h in range(heads):
        lanes = head(h)
        v_lanes = slice(width + h * DH, width + (h + 1) * DH)
        for a in range(blocks):
            near = (a + 1) * BLK
            here = slice(a * BLK, near)
            keys, values = [krot_ref[:near, lanes]], [value_ref[:near, lanes]]
            for l in range(MAXL):
                e = a * MAXL + l
                raw = far_keys[e, :, lanes]
                keys.append((nn(raw, hi_ref[e, h]) + nn(raw, lo_ref[e, h])).astype(BF16))
                values.append(far_values[e, :, lanes])
            keys, values = jnp.concatenate(keys, axis=0), jnp.concatenate(values, axis=0)
            qrot, grad = qrot_ref[here, lanes], grad_ref[here, lanes]
            scores = nt(keys, qrot) * scaling
            shape = scores.shape
            row, col = iota(shape, 0), iota(shape, 1)
            hidden = (row < near) & (row - a * BLK > col)
            scores = jnp.where(hidden, -jnp.inf, scores)
            top = jnp.max(scores, axis=0, keepdims=True)
            weight = jnp.exp(scores - top)
            probs = weight * (1.0 / jnp.sum(weight, axis=0, keepdims=True))
            probs_b = probs.astype(BF16)
            dprobs = nt(values, grad)
            delta = jnp.sum(probs_b.astype(F32) * dprobs, axis=0, keepdims=True)
            dscores = (probs * (dprobs - delta)).astype(BF16)
            dq_rot = tn(dscores, keys) * scaling
            dq_top, dq_low = split(dq_rot)
            dq_ref[here, lanes] = nt(dq_top, local_ref[a, h]).astype(BF16)
            query = query_ref[here, lanes]
            dcum_ref[a, h] = tn(query, dq_top) + tn(query, dq_low)
            dkeys = nn(dscores, qrot) * scaling
            dvalues = nn(probs_b, grad)
            if a > 0:
                dk_ref[: near - BLK, lanes] += dkeys[: near - BLK]
                dv_ref[: near - BLK, lanes] += dvalues[: near - BLK]
            dk_ref[here, lanes] = dkeys[near - BLK : near]
            dv_ref[here, lanes] = dvalues[near - BLK : near]
            for l in range(MAXL):
                e = a * MAXL + l
                part = slice(near + l * BLK, near + (l + 1) * BLK)
                part_k, part_v = dkeys[part].astype(BF16), dvalues[part].astype(BF16)
                if pieces:
                    distance = owners_ref[a, l] ^ me_ref[0]
                    spot = (distance & 1) * blocks + offsets_ref[a, l]
                    chip = distance >> 1
                    payload[spot, chip, :, lanes] += part_k
                    payload[spot, chip, :, v_lanes] += part_v
                else:
                    outs[0][e, :, lanes] = part_k
                    outs[0][e, :, v_lanes] = part_v
    if pieces:
        copies = [
            pltpu.make_async_copy(payload.at[i], outs[i], out_sems.at[i]) for i in range(pieces)
        ]
        for copy in copies:
            copy.start()
        for copy in copies:
            copy.wait()


def run_attend(me, owners, offsets, key_srcs, value_srcs, arrays, heads, blocks, pieces):
    rows, width = arrays[0].shape
    entries = blocks * MAXL
    sources = len(key_srcs)
    any_spec = pl.BlockSpec(memory_space=pl.ANY)
    smem = [pl.BlockSpec(memory_space=pltpu.SMEM)] * 3
    scratch = [
        pltpu.VMEM((entries, BLK, width), BF16),
        pltpu.VMEM((entries, BLK, width), BF16),
        pltpu.SemaphoreType.DMA((2, entries)),
    ]
    if pieces:
        chips = sources // 2
        out_parts = [jax.ShapeDtypeStruct((chips, BLK, 2 * width), BF16)] * pieces
        part_specs = [any_spec] * pieces
        scratch += [
            pltpu.VMEM((pieces, chips, BLK, 2 * width), BF16),
            pltpu.SemaphoreType.DMA((pieces,)),
        ]
    else:
        out_parts = [jax.ShapeDtypeStruct((entries, BLK, 2 * width), BF16)]
        part_specs = in_vmem(1)
    return pl.pallas_call(
        functools.partial(attend_kernel, heads, blocks, sources, pieces),
        out_shape=[
            jax.ShapeDtypeStruct((rows, width), BF16),
            jax.ShapeDtypeStruct((blocks, heads, DH, DH), F32),
            jax.ShapeDtypeStruct((rows, width), F32),
            jax.ShapeDtypeStruct((rows, width), F32),
        ]
        + out_parts,
        in_specs=smem + [any_spec] * (2 * sources) + in_vmem(8),
        out_specs=in_vmem(4) + part_specs,
        scratch_shapes=scratch,
        compiler_params=compiler_params(),
        name="attend",
    )(me, owners, offsets, *key_srcs, *value_srcs, *arrays)


def project_kernel(heads, parts, *refs):
    part_refs = refs[:parts]
    dk_loc, dv_loc, dq_ref, key_ref, dcum_in, cum_ref, wq, wk, wv = refs[parts : parts + 9]
    out_ref, dcum_out, dk_ref, dv_ref = refs[parts + 9 :]
    width = heads * DH

    @pl.when(pl.program_id(0) == 0)
    def _():
        total = part_refs[0][...].astype(F32)
        for ref in part_refs[1:]:
            total = total + ref[...].astype(F32)
        dv_ref[...] = (dv_loc[...] + total[:, width:]).astype(BF16)
        for h in range(heads):
            dk_rot = dk_loc[:, head(h)] + total[:, head(h)]
            dk_top, dk_low = split(dk_rot)
            dk_ref[:, head(h)] = nt(dk_top, cum_ref[0, h]).astype(BF16)
            key = key_ref[:, head(h)]
            dcum_out[h] = dcum_in[0, h] + tn(key, dk_top) + tn(key, dk_low)

    term = nt(dq_ref[...], wq[...]) + nt(dk_ref[...], wk[...]) + nt(dv_ref[...], wv[...])
    out_ref[0] = term.astype(BF16)


def run_project(block, parts, dk_loc, dv_loc, dq, key_rows, dcum, cum, weights, heads, groups):
    width = heads * DH
    model = weights[0].shape[0]
    chunk = model // groups
    tile = min(512, chunk)
    per = chunk // tile
    rows_spec = pl.BlockSpec((BLK, width), lambda t: (block, 0))
    part_spec = pl.BlockSpec((BLK, 2 * width), lambda t: (0, 0))
    head_spec = pl.BlockSpec((1, heads, DH, DH), lambda t: (block, 0, 0, 0))
    weight_spec = pl.BlockSpec((tile, width), lambda t: (t, 0))
    return pl.pallas_call(
        functools.partial(project_kernel, heads, len(parts)),
        grid=(model // tile,),
        out_shape=[
            jax.ShapeDtypeStruct((groups, BLK, chunk), BF16),
            jax.ShapeDtypeStruct((heads, DH, DH), F32),
        ],
        in_specs=[part_spec] * len(parts)
        + [rows_spec] * 4
        + [head_spec] * 2
        + [weight_spec] * 3,
        out_specs=[
            pl.BlockSpec((1, BLK, tile), lambda t: (t // per, 0, t % per)),
            pl.BlockSpec((heads, DH, DH), lambda t: (0, 0, 0)),
        ],
        scratch_shapes=[pltpu.VMEM((BLK, width), BF16), pltpu.VMEM((BLK, width), BF16)],
        compiler_params=compiler_params(),
        cost_estimate=pl.CostEstimate(
            flops=6 * BLK * model * width, bytes_accessed=6 * model * width, transcendentals=0
        ),
        name="project",
    )(*parts, dk_loc, dv_loc, dq, key_rows, dcum, cum, *weights)


def adjoint_kernel(heads, blocks, base_ref, *refs):
    dcums = refs[:blocks]
    unit_ref, rows_ref, inv_ref, out_ref = refs[blocks:]
    count, width = unit_ref.shape
    square = (count, count)
    eye = (iota(square, 0) == iota(square, 1)).astype(F32)
    row, col = iota(square, 0), iota(square, 1)
    for h in range(heads):
        units, rows, inverse = unit_ref[:, head(h)], rows_ref[:, head(h)], inv_ref[h]
        inverse_t = nt_high(eye, inverse)
        x_total = jnp.zeros((count, DH), F32)
        y_total = jnp.zeros((count, DH), F32)
        for j in range(blocks):
            mine = base_ref[0] * blocks + j
            dcum = dcums[j][h]
            live = iota((count, 1), 0) <= mine
            moved = nt_high(rows, dcum)
            overlap = jnp.where(col <= mine, nt_high(moved, units), 0.0)
            gamma = nn_high(overlap, inverse)
            gamma = jnp.where((row < col) & (col <= mine), gamma, 0.0)
            x_total += jnp.where(live, moved - 2.0 * nn_high(gamma, units), 0.0)
            beta = jnp.where(col <= mine, eye - inverse_t, 0.0)
            turned = jnp.where(live, units - nn_high(beta, units), 0.0)
            y_total += nn_high(turned, dcum)
        out_ref[:, head(h)] = x_total
        out_ref[:, slice(width + h * DH, width + (h + 1) * DH)] = y_total


def run_adjoint(me, dcums, unit, rows, inverse, heads, blocks):
    count, width = unit.shape
    return pl.pallas_call(
        functools.partial(adjoint_kernel, heads, blocks),
        out_shape=jax.ShapeDtypeStruct((count, 2 * width), F32),
        in_specs=[pl.BlockSpec(memory_space=pltpu.SMEM)] + in_vmem(blocks + 3),
        out_specs=pl.BlockSpec(memory_space=pltpu.VMEM),
        compiler_params=compiler_params(),
        name="adjoint",
    )(me, *dcums, unit, rows, inverse)


def house_kernel(heads, blocks, base_ref, got_ref, unit_ref, rows_ref, house_ref, out_ref):
    count, width = unit_ref.shape
    total = jnp.sum(got_ref[...], axis=0)
    for h in range(heads):
        x_part = total[:, head(h)]
        y_part = total[:, slice(width + h * DH, width + (h + 1) * DH)]
        along = nt_high(y_part, rows_ref[:, head(h)])
        spot = iota((blocks, count), 0) + base_ref[0] * blocks
        along = jnp.where(iota((blocks, count), 1) < spot, along, 0.0)
        turned = y_part - 2.0 * nn_high(along, unit_ref[:, head(h)])
        dunit = -2.0 * (x_part + turned)
        house = house_ref[:, head(h)]
        lengths = jnp.sqrt(jnp.sum(house * house, axis=1, keepdims=True) + 1e-06)
        unit = house / lengths
        inner = jnp.sum(unit * dunit, axis=1, keepdims=True)
        out_ref[:, head(h)] = (dunit - unit * inner) / lengths


def run_house(me, got, unit, rows, house_dirs, heads, blocks):
    return pl.pallas_call(
        functools.partial(house_kernel, heads, blocks),
        out_shape=jax.ShapeDtypeStruct(house_dirs.shape, F32),
        in_specs=[pl.BlockSpec(memory_space=pltpu.SMEM)] + in_vmem(4),
        out_specs=pl.BlockSpec(memory_space=pltpu.VMEM),
        compiler_params=compiler_params(),
        name="house_grad",
    )(me, got, unit, rows, house_dirs)


def hop(value, distance, count):
    return lax.ppermute(value, "ctx", [(i, i ^ distance) for i in range(count)])


def shards(
    query_rows, key_rows, value_rows, grad_out, house_dirs, owners, offsets, w_query, w_key, w_value
):
    tok_rows, width = query_rows.shape
    heads, blocks = width // DH, tok_rows // BLK
    ctx_count, groups = lax.axis_size("ctx"), lax.axis_size("head")
    my_index = lax.axis_index("ctx")
    me = my_index.astype(jnp.int32).reshape(1)
    by_hand = ctx_count == 8
    core, across, along = 1, 2, 4

    if by_hand:
        pieces_house = [house_dirs] + [hop(house_dirs, r, 8) for r in range(1, 8)]
        order = jnp.arange(8) ^ my_index
        house_all = jnp.stack(pieces_house)[order].reshape(8 * blocks, width)
        key_y, value_x = hop(key_rows, along, 8), hop(value_rows, across, 8)
        key_x, value_y = hop(key_rows, across, 8), hop(value_rows, along, 8)
        key_d, value_d = hop(key_y, across, 8), hop(value_x, along, 8)
        keys = [key_rows, key_x, key_y, key_d]
        values = [value_rows, value_x, value_y, value_d]
        key_srcs = [part for key in keys for part in (key, hop(key, core, 8))]
        value_srcs = [part for value in values for part in (value, hop(value, core, 8))]
    else:
        house_all = lax.all_gather(house_dirs, "ctx", axis=0, tiled=True)
        key_srcs = [lax.all_gather(key_rows, "ctx")]
        value_srcs = [lax.all_gather(value_rows, "ctx")]

    unit, rows, inverse, qrot, krot, local, list_hi, list_lo = run_chain(
        me, owners, offsets, house_all, query_rows, key_rows, heads, blocks
    )
    pieces = 2 * blocks if by_hand else 0
    dq, dcum, dk_loc, dv_loc, *outs = run_attend(
        me,
        owners,
        offsets,
        key_srcs,
        value_srcs,
        (query_rows, qrot, krot, value_rows, grad_out, local, list_hi, list_lo),
        heads,
        blocks,
        pieces,
    )
    if not by_hand:
        spots = (owners * blocks + offsets).reshape(-1)
        empty = jnp.zeros((ctx_count * blocks, BLK, 2 * width), BF16)
        filled = empty.at[spots].add(outs[0])
        back = lax.psum_scatter(filled, "ctx", scatter_dimension=0, tiled=True)

    weights = (w_query, w_key, w_value)
    shares, dcums = [], []
    for j in range(blocks):
        if by_hand:
            near = outs[j] + hop(outs[blocks + j], core, 8)
            far_k = hop(near[3, :, :width], across, 8)
            far_v = hop(near[3, :, width:], along, 8)
            to_x = jnp.concatenate([near[1, :, :width], near[1, :, width:] + far_v], axis=1)
            to_y = jnp.concatenate([near[2, :, :width] + far_k, near[2, :, width:]], axis=1)
            parts = [near[0], hop(to_x, across, 8), hop(to_y, along, 8)]
        else:
            parts = [back[j]]
        term, dcum_j = run_project(
            j, parts, dk_loc, dv_loc, dq, key_rows, dcum, local, weights, heads, groups
        )
        dcums.append(dcum_j)
        shares.append(lax.psum_scatter(term, "head", scatter_dimension=0, tiled=False))

    sums = run_adjoint(me, dcums, unit, rows, inverse, heads, blocks)
    sums = sums.reshape(ctx_count, blocks, 2 * width)
    got = lax.all_to_all(sums, "ctx", split_axis=0, concat_axis=0, tiled=True)
    house_grad = run_house(me, got, unit, rows, house_dirs, heads, blocks)
    return (jnp.concatenate(shares, axis=0), house_grad)


def solution(mesh):
    placed = (
        P("ctx", "head"),
        P("ctx", "head"),
        P("ctx", "head"),
        P("ctx", "head"),
        P("ctx", "head"),
        P("ctx", None),
        P("ctx", None),
        P(None, "head"),
        P(None, "head"),
        P(None, "head"),
    )
    return jax.shard_map(
        shards,
        mesh=mesh,
        in_specs=placed,
        out_specs=(P("ctx", "head"), P("ctx", "head")),
        check_vma=False,
    )
```

time: 315 us -> 254 us (0.81); the launches traced: 310 us -> 253 us
  matrix products: 101 us -> 0 us
  Pallas kernels: 0 us -> 93 us
  local copies, waits for them, and re-layouts: 70.8 us -> 6.63 us
  starting transfers between devices: 18.5 us -> 32.2 us
  waiting for transfers between devices: 76.5 us -> 89.7 us
  blocking collectives: 19.2 us -> 8.01 us
    dot_general x53 -> x0, matrix products: 101 us -> none  [the longest x3 22.8 us: shards(): lax.dot_general(weight_mat, grad_mat, (((1,), (1,)), ((), ())), preferred...]
    pallas_call x0 -> x8, Pallas kernels: none -> 93 us  [the longest x4 43.2 us: run_project(): pl.pallas_call(functools.partial(project_kernel, heads, len(parts)), grid...]
    ppermute x0 -> x41, waiting for transfers between devices: none -> 79.1 us  [hop(): return lax.ppermute(value, 'ctx', [(i, i ^ distance) for i in range(count)])]
    reduce_scatter x1 -> x4, waiting for transfers between devices: 48.5 us -> 10.6 us  [shards(): lax.psum_scatter(term, 'head', scatter_dimension=0, tiled=False)]
    ppermute x0 -> x41, starting transfers between devices: none -> 32.1 us  [hop(): return lax.ppermute(value, 'ctx', [(i, i ^ distance) for i in range(count)])]
    all_to_all x4 -> x0, waiting for transfers between devices: 24.1 us -> none  [the longest x1 13.5 us: shards(): lax.all_to_all(sent_keys, 'ctx', split_axis=0, concat_axis=0, tiled=True)]
    all_gather x2 -> x0, blocking collectives: 19.2 us -> none  [the longest x1 10.3 us: shards(): lax.all_gather(owners, 'ctx', axis=0, tiled=True)]
    reshape x15 -> x2, local copies, waits for them, and re-layouts: 18.6 us -> 0.07 us  [the longest x1 0.05 us: shards(): sums = sums.reshape(ctx_count, blocks, 2 * width)]
  transfers between devices with their start and end apart: 8 -> 45, of which waited for: 5 -> 24; matrix products, arithmetic and copies ran while one was open for 54% -> 3% of each run, Pallas kernels for 0% -> 28%
where the time goes in v1:
time: 254 us; the launch traced here: 253 us
  Pallas kernels  93 us (37%)
  waiting for transfers between devices  89.7 us (35%)
  starting transfers between devices  32.2 us (13%)
  between operations  14.1 us (6%)
  other arithmetic  8.99 us (4%)
  blocking collectives  8.01 us (3%)
  local copies, waits for them, and re-layouts  6.63 us (3%)
    ppermute x41, waiting for transfers between devices, hop(): return lax.ppermute(value, 'ctx', [(i, i ^ distance) for i in range(count)])  79.1 us
    pallas_call x4, Pallas kernels, run_project(): pl.pallas_call(functools.partial(project_kernel, heads, len(parts)), grid...  43.2 us
    ppermute x41, starting transfers between devices, hop(): return lax.ppermute(value, 'ctx', [(i, i ^ distance) for i in range(count)])  32.1 us
    pallas_call x1, Pallas kernels, run_attend(): pl.pallas_call(functools.partial(attend_kernel, heads, blocks, sources, p...  22.6 us
    pallas_call x1, Pallas kernels, run_chain(): pl.pallas_call(functools.partial(chain_kernel, heads, blocks), out_shape=...  14.5 us
    pallas_call x1, Pallas kernels, run_adjoint(): pl.pallas_call(functools.partial(adjoint_kernel, heads, blocks), out_shap...  11 us
    reduce_scatter x4, waiting for transfers between devices, shards(): lax.psum_scatter(term, 'head', scatter_dimension=0, tiled=False)  10.6 us
    all_to_all x1, blocking collectives, shards(): got = lax.all_to_all(sums, 'ctx', split_axis=0, concat_axis=0, tiled=True)  8.01 us
  transfers between devices with their start and end apart: 45, of which 24 were waited for; matrix products, arithmetic and copies ran while one was open for 3% of the time, Pallas kernels for 28%

profile of v1, /device:TPU:0, one launch (start us, length us, event | category | flops | bytes accessed | tf_op | source)
XLA Modules:
  0.0 252.7 jit_solution(15097995041691707898)
XLA Ops:
  7.2 4.0 %collective-permute-start.19 = (f32[4,512]{1,0:T(4,128)}, f32[4,512]{1,0:T(4,128)S(1)}, u32[]{:S(2)}, u32[]{:S(2)}) collective-permute-start(f32[4,512]{1,0:T(4,128)} %house_ref.1), channel_id=1, source_target_pairs={{0,24},{4,28},{8,16},{12,20},{16,8},{20,12},{24,0},{28,4},{1,25},{... | collective-permute-start | bytes 24584 | tf_op jit(solution)/shard_map/ppermute | solution.py:435
  18.0 9.4 %collective-permute-done.15 = f32[4,512]{1,0:T(4,128)S(1)} collective-permute-done((f32[4,512]{1,0:T(4,128)}, f32[4,512]{1,0:T(4,128)S(1)}, u32[]{:S(2)}, u32[]{:S(2)}) %collective-permute-start.15) | collective-permute-done | bytes 8224 | tf_op jit(solution)/shard_map/ppermute | solution.py:435
  30.7 2.5 collective-permute-done.20
  35.7 5.5 %collective-permute-done.3.refs_7_ = bf16[512,512]{1,0:T(8,128)(2,1)} collective-permute-done((bf16[512,512]{1,0:T(8,128)(2,1)}, bf16[512,512]{1,0:T(8,128)(2,1)}, u32[]{:S(2)}, u32[]{:S(2)}) %collective-permute-start.3) | collective-permute-done | bytes 524320 | tf_op jit(solution)/shard_map/ppermute | solution.py:435
  41.8 6.5 %collective-permute-done.1.refs_5_ = bf16[512,512]{1,0:T(8,128)(2,1)} collective-permute-done((bf16[512,512]{1,0:T(8,128)(2,1)}, bf16[512,512]{1,0:T(8,128)(2,1)}, u32[]{:S(2)}, u32[]{:S(2)}) %collective-permute-start.1) | collective-permute-done | bytes 524320 | tf_op jit(solution)/shard_map/ppermute | solution.py:435
  48.8 3.2 %collective-permute-done.12.refs_17_ = bf16[512,512]{1,0:T(8,128)(2,1)} collective-permute-done((bf16[512,512]{1,0:T(8,128)(2,1)S(1)}, bf16[512,512]{1,0:T(8,128)(2,1)}, u32[]{:S(2)}, u32[]{:S(2)}) %collective-permute-start.12) | collective-permute-done | bytes 524320 | tf_op jit(solution)/shard_map/ppermute | solution.py:435
  52.5 6.6 %collective-permute-done.5.refs_9_ = bf16[512,512]{1,0:T(8,128)(2,1)} collective-permute-done((bf16[512,512]{1,0:T(8,128)(2,1)}, bf16[512,512]{1,0:T(8,128)(2,1)}, u32[]{:S(2)}, u32[]{:S(2)}) %collective-permute-start.5) | collective-permute-done | bytes 524320 | tf_op jit(solution)/shard_map/ppermute | solution.py:435
  59.8 14.5 %house_chain.1 = (f32[32,512]{1,0:T(8,128)S(1)}, f32[32,512]{1,0:T(8,128)S(1)}, f32[4,32,32]{2,1,0:T(8,128)S(1)}, bf16[512,512]{1,0:T(8,128)(2,1)S(1)}, bf16[512...) custom-call(s32[1]{0:T(128)} %bitcast.base_ref.refs_0_, ...), custom_call_target="tpu_custom_call" | custom-call | tf_op jit(solution)/shard_map/house_chain/pallas_call | solution.py:144
  77.8 22.6 %attend.1 = (bf16[512,512]{1,0:T(8,128)(2,1)S(1)}, f32[4,4,128,128]{3,2,1,0:T(8,128)}, f32[512,512]{1,0:T(8,128)}, f32[512,512]{1,0:T(8,128)}, bf16[4,128,1024]{...) custom-call(s32[1]{0:T(128)} %bitcast.base_ref.refs_0_, ...), custom_call_target="tpu_custom_call" | custom-call | tf_op jit(solution)/shard_map/attend/pallas_call | solution.py:291
  107.4 3.7 %collective-permute-done.24 = bf16[128,512]{1,0:T(8,128)(2,1)S(1)} collective-permute-done((bf16[128,512]{1,0:T(8,128)(2,1)S(1)}, bf16[128,512]{1,0:T(8,128)(2,1)S(1)}, u32[]{:S(2)}, u32[]{:S(2)}) %collective-permute-start.24) | collective-permute-done | bytes 131104 | tf_op jit(solution)/shard_map/ppermute | solution.py:435
  113.7 5.9 %collective-permute-done.23.refs_1_ = bf16[128,1024]{1,0:T(8,128)(2,1)S(1)} collective-permute-done((bf16[128,1024]{1,0:T(8,128)(2,1)S(1)}, bf16[128,1024]{1,0:T(8,128)(2,1)S(1)}, u32[]{:S(2)}, u32[]{:S(2)}) %collective-permute-start.23) | collective-permute-done | bytes 262176 | tf_op jit(solution)/shard_map/ppermute | solution.py:435
  120.3 10.8 %project.4 = (bf16[4,128,1024]{2,1,0:T(8,128)(2,1)}, f32[4,128,128]{2,1,0:T(8,128)S(1)}) custom-call(bf16[128,1024]{1,0:T(8,128)(2,1)S(1)} %slice_bitcast_fusion.3.refs_0_, bf16[128,1024]{1,0:T(8,128)(2,1)S(1)} %collective-permute-done.23.refs_1_, bf16[128,1024]{1,0:T(8,128)(2,1)S(1)} %collective-permute-done.25.refs_2_, ...), custom_call_target="tpu_custom_call" | custom-call | flops 1610612736 | bytes 12582912 | tf_op jit(solution)/shard_map/project/pallas_call | solution.py:341
  135.0 2.9 %collective-permute-done.29 = bf16[128,512]{1,0:T(8,128)(2,1)S(1)} collective-permute-done((bf16[128,512]{1,0:T(8,128)(2,1)S(1)}, bf16[128,512]{1,0:T(8,128)(2,1)S(1)}, u32[]{:S(2)}, u32[]{:S(2)}) %collective-permute-start.29) | collective-permute-done | bytes 131104 | tf_op jit(solution)/shard_map/ppermute | solution.py:435
  140.9 4.6 %collective-permute-done.28.refs_1_ = bf16[128,1024]{1,0:T(8,128)(2,1)S(1)} collective-permute-done((bf16[128,1024]{1,0:T(8,128)(2,1)S(1)}, bf16[128,1024]{1,0:T(8,128)(2,1)S(1)}, u32[]{:S(2)}, u32[]{:S(2)}) %collective-permute-start.28) | collective-permute-done | bytes 262176 | tf_op jit(solution)/shard_map/ppermute | solution.py:435
  146.5 10.8 %project.5 = (bf16[4,128,1024]{2,1,0:T(8,128)(2,1)}, f32[4,128,128]{2,1,0:T(8,128)S(1)}) custom-call(bf16[128,1024]{1,0:T(8,128)(2,1)S(1)} %slice_bitcast_fusion.2.refs_0_, bf16[128,1024]{1,0:T(8,128)(2,1)S(1)} %collective-permute-done.28.refs_1_, bf16[128,1024]{1,0:T(8,128)(2,1)S(1)} %collective-permute-done.30.refs_2_, ...), custom_call_target="tpu_custom_call" | custom-call | flops 1610612736 | bytes 12582912 | tf_op jit(solution)/shard_map/project/pallas_call | solution.py:341
  161.2 4.2 %collective-permute-done.34 = bf16[128,512]{1,0:T(8,128)(2,1)S(1)} collective-permute-done((bf16[128,512]{1,0:T(8,128)(2,1)S(1)}, bf16[128,512]{1,0:T(8,128)(2,1)S(1)}, u32[]{:S(2)}, u32[]{:S(2)}) %collective-permute-start.34) | collective-permute-done | bytes 131104 | tf_op jit(solution)/shard_map/ppermute | solution.py:435
  168.5 4.6 %collective-permute-done.33.refs_1_ = bf16[128,1024]{1,0:T(8,128)(2,1)S(1)} collective-permute-done((bf16[128,1024]{1,0:T(8,128)(2,1)S(1)}, bf16[128,1024]{1,0:T(8,128)(2,1)S(1)}, u32[]{:S(2)}, u32[]{:S(2)}) %collective-permute-start.33) | collective-permute-done | bytes 262176 | tf_op jit(solution)/shard_map/ppermute | solution.py:435
  174.1 10.8 %project.6 = (bf16[4,128,1024]{2,1,0:T(8,128)(2,1)}, f32[4,128,128]{2,1,0:T(8,128)S(1)}) custom-call(bf16[128,1024]{1,0:T(8,128)(2,1)S(1)} %slice_bitcast_fusion.1.refs_0_, bf16[128,1024]{1,0:T(8,128)(2,1)S(1)} %collective-permute-done.33.refs_1_, bf16[128,1024]{1,0:T(8,128)(2,1)S(1)} %collective-permute-done.35.refs_2_, ...), custom_call_target="tpu_custom_call" | custom-call | flops 1610612736 | bytes 12582912 | tf_op jit(solution)/shard_map/project/pallas_call | solution.py:341
  188.8 4.3 %collective-permute-done.39 = bf16[128,512]{1,0:T(8,128)(2,1)S(1)} collective-permute-done((bf16[128,512]{1,0:T(8,128)(2,1)S(1)}, bf16[128,512]{1,0:T(8,128)(2,1)S(1)}, u32[]{:S(2)}, u32[]{:S(2)}) %collective-permute-start.39) | collective-permute-done | bytes 131104 | tf_op jit(solution)/shard_map/ppermute | solution.py:435
  196.1 4.6 %collective-permute-done.38.refs_1_ = bf16[128,1024]{1,0:T(8,128)(2,1)S(1)} collective-permute-done((bf16[128,1024]{1,0:T(8,128)(2,1)S(1)}, bf16[128,1024]{1,0:T(8,128)(2,1)S(1)}, u32[]{:S(2)}, u32[]{:S(2)}) %collective-permute-start.38) | collective-permute-done | bytes 262176 | tf_op jit(solution)/shard_map/ppermute | solution.py:435
  201.8 10.8 %project.7 = (bf16[4,128,1024]{2,1,0:T(8,128)(2,1)}, f32[4,128,128]{2,1,0:T(8,128)S(1)}) custom-call(bf16[128,1024]{1,0:T(8,128)(2,1)S(1)} %slice_bitcast_fusion.refs_0_, bf16[128,1024]{1,0:T(8,128)(2,1)S(1)} %collective-permute-done.38.refs_1_, bf16[128,1024]{1,0:T(8,128)(2,1)S(1)} %collective-permute-done.40.refs_2_, ...), custom_call_target="tpu_custom_call" | custom-call | flops 1610612736 | bytes 12582912 | tf_op jit(solution)/shard_map/project/pallas_call | solution.py:341
  212.6 11.0 %adjoint.1 = f32[32,1024]{1,0:T(8,128)S(1)} custom-call(s32[1]{0:T(128)} %bitcast.base_ref.refs_0_, f32[4,128,128]{2,1,0:T(8,128)S(1)} %get-tuple-element.51.refs_0_, f32[4,128,128]{2,1,0:T(8,128)S(1)} %get-tuple-element.52.refs_1_, f32[4,128,128]{2,1,0:T(8,128)S(1)} %get-tuple-element.53.refs_2_, f32[4,128,128]{2,1,0:T(8,128)S(1)} %get-tuple-element.54.refs_3_, ...), custom_call_target="tpu_custom_call" | custom-call | tf_op jit(solution)/shard_map/adjoint/pallas_call | solution.py:395
  223.7 8.0 %all_to_all.5.got_ref = f32[8,4,1024]{2,1,0:T(4,128)S(1)} all-to-all(f32[8,4,1024]{2,1,0:T(4,128)S(1)} %reshape.31), channel_id=1, replica_groups=mesh['ctx'=8,'head'=4] {'ctx'}, dimensions={0} | all-to-all | bytes 262144 | tf_op jit(solution)/shard_map/all_to_all | solution.py:506
  233.3 10.6 %reduce-scatter.11.cloned.1.call-done = bf16[1,128,1024]{2,1,0:T(8,128)(2,1)} async-done(((bf16[4,128,1024]{2,1,0:T(8,128)(2,1)}), bf16[1,128,1024]{2,1,0:T(8,128)(2,1)}) %reduce-scatter.11.cloned.1.call-update) | async-done | bytes 262160 | tf_op jit(solution)/shard_map/reduce_scatter | solution.py:502
  (143 shorter events, 56.1 us)
Async XLA Ops:
  7.2 226.2 %reduce-scatter.5.cloned.1.call-start = ((), (), s32[]{:S(2)}) async-start(), calls=%async_computation.5 | async-start | bytes 1310720 | tf_op jit(solution)/shard_map/reduce_scatter | solution.py:502
  7.2 7.5 %collective-permute-start.19 = (f32[4,512]{1,0:T(4,128)}, f32[4,512]{1,0:T(4,128)S(1)}, u32[]{:S(2)}, u32[]{:S(2)}) collective-permute-start(f32[4,512]{1,0:T(4,128)} %house_ref.1), channel_id=1, source_target_pairs={{0,24},{4,28},{8,16},{12,20},{16,8},{20,12},{24,0},{28,4},{1,25},{... | collective-permute-start | bytes 24584 | tf_op jit(solution)/shard_map/ppermute | solution.py:435
  13.2 21.4 %collective-permute-start.8 = (bf16[512,512]{1,0:T(8,128)(2,1)}, bf16[512,512]{1,0:T(8,128)(2,1)S(1)}, u32[]{:S(2)}, u32[]{:S(2)}) collective-permute-start(bf16[512,512]{1,0:T(8,128)(2,1)} %refs_22_.1), channel_id=1, source_target_pairs={{0,8},{4,12},{8,0},{12,4},{16,24},{20,28},{24,16},{28,20},{1,9},{5... | collective-permute-start | bytes 1572872 | tf_op jit(solution)/shard_map/ppermute | solution.py:435
  14.7 20.1 %collective-permute-start.7 = (bf16[512,512]{1,0:T(8,128)(2,1)}, bf16[512,512]{1,0:T(8,128)(2,1)S(1)}, u32[]{:S(2)}, u32[]{:S(2)}) collective-permute-start(bf16[512,512]{1,0:T(8,128)(2,1)} %refs_22_.1), channel_id=1, source_target_pairs={{0,4},{4,0},{8,12},{12,8},{16,20},{20,16},{24,28},{28,24},{1,5},{5... | collective-permute-start | bytes 1572872 | tf_op jit(solution)/shard_map/ppermute | solution.py:435
  14.7 21.0 %collective-permute-start.10 = (bf16[512,512]{1,0:T(8,128)(2,1)}, bf16[512,512]{1,0:T(8,128)(2,1)S(1)}, u32[]{:S(2)}, u32[]{:S(2)}) collective-permute-start(bf16[512,512]{1,0:T(8,128)(2,1)} %refs_22_.1), channel_id=1, source_target_pairs={{0,16},{4,20},{8,24},{12,28},{16,0},{20,4},{24,8},{28,12},{1,17},{... | collective-permute-start | bytes 1572872 | tf_op jit(solution)/shard_map/ppermute | solution.py:435
  15.2 25.9 %collective-permute-start.3 = (bf16[512,512]{1,0:T(8,128)(2,1)}, bf16[512,512]{1,0:T(8,128)(2,1)}, u32[]{:S(2)}, u32[]{:S(2)}) collective-permute-start(bf16[512,512]{1,0:T(8,128)(2,1)} %refs_6_.7), channel_id=1, source_target_pairs={{0,16},{4,20},{8,24},{12,28},{16,0},{20,4},{24,8},{28,12},{1,17},{... | collective-permute-start | bytes 1572872 | tf_op jit(solution)/shard_map/ppermute | solution.py:435
  17.5 9.9 %collective-permute-start.15 = (f32[4,512]{1,0:T(4,128)}, f32[4,512]{1,0:T(4,128)S(1)}, u32[]{:S(2)}, u32[]{:S(2)}) collective-permute-start(f32[4,512]{1,0:T(4,128)} %house_ref.1), channel_id=1, source_target_pairs={{0,8},{4,12},{8,0},{12,4},{16,24},{20,28},{24,16},{28,20},{1,9},{5... | collective-permute-start | bytes 24584 | tf_op jit(solution)/shard_map/ppermute | solution.py:435
  33.2 15.0 %collective-permute-start.1 = (bf16[512,512]{1,0:T(8,128)(2,1)}, bf16[512,512]{1,0:T(8,128)(2,1)}, u32[]{:S(2)}, u32[]{:S(2)}) collective-permute-start(bf16[512,512]{1,0:T(8,128)(2,1)} %refs_6_.7), channel_id=1, source_target_pairs={{0,8},{4,12},{8,0},{12,4},{16,24},{20,28},{24,16},{28,20},{1,9},{5... | collective-permute-start | bytes 1572872 | tf_op jit(solution)/shard_map/ppermute | solution.py:435
  34.6 13.7 %collective-permute-start = (bf16[512,512]{1,0:T(8,128)(2,1)}, bf16[512,512]{1,0:T(8,128)(2,1)S(1)}, u32[]{:S(2)}, u32[]{:S(2)}) collective-permute-start(bf16[512,512]{1,0:T(8,128)(2,1)} %refs_6_.7), channel_id=1, source_target_pairs={{0,4},{4,0},{8,12},{12,8},{16,20},{20,16},{24,28},{28,24},{1,5},{5... | collective-permute-start | bytes 1572872 | tf_op jit(solution)/shard_map/ppermute | solution.py:435
  34.8 17.2 %collective-permute-start.12 = (bf16[512,512]{1,0:T(8,128)(2,1)S(1)}, bf16[512,512]{1,0:T(8,128)(2,1)}, u32[]{:S(2)}, u32[]{:S(2)}) collective-permute-start(bf16[512,512]{1,0:T(8,128)(2,1)S(1)} %collective-permute-done.8.refs_13_), channel_id=1, source_target_pairs={{0,16},{4,20},{8,24},{12,28},{16,0},{20,4},{24,8},{28,12},{1,17},{... | collective-permute-start | bytes 1572872 | tf_op jit(solution)/shard_map/ppermute | solution.py:435
  35.7 16.3 %collective-permute-start.9 = (bf16[512,512]{1,0:T(8,128)(2,1)S(1)}, bf16[512,512]{1,0:T(8,128)(2,1)S(1)}, u32[]{:S(2)}, u32[]{:S(2)}) collective-permute-start(bf16[512,512]{1,0:T(8,128)(2,1)S(1)} %collective-permute-done.8.refs_13_), channel_id=1, source_target_pairs={{0,4},{4,0},{8,12},{12,8},{16,20},{20,16},{24,28},{28,24},{1,5},{5... | collective-permute-start | bytes 1572872 | tf_op jit(solution)/shard_map/ppermute | solution.py:435
  41.2 17.9 %collective-permute-start.5 = (bf16[512,512]{1,0:T(8,128)(2,1)}, bf16[512,512]{1,0:T(8,128)(2,1)}, u32[]{:S(2)}, u32[]{:S(2)}) collective-permute-start(bf16[512,512]{1,0:T(8,128)(2,1)} %collective-permute-done.3.refs_7_), channel_id=1, source_target_pairs={{0,8},{4,12},{8,0},{12,4},{16,24},{20,28},{24,16},{28,20},{1,9},{5... | collective-permute-start | bytes 1572872 | tf_op jit(solution)/shard_map/ppermute | solution.py:435
  48.2 28.4 %collective-permute-start.4 = (bf16[512,512]{1,0:T(8,128)(2,1)}, bf16[512,512]{1,0:T(8,128)(2,1)}, u32[]{:S(2)}, u32[]{:S(2)}) collective-permute-start(bf16[512,512]{1,0:T(8,128)(2,1)} %collective-permute-done.3.refs_7_), channel_id=1, source_target_pairs={{0,4},{4,0},{8,12},{12,8},{16,20},{20,16},{24,28},{28,24},{1,5},{5... | collective-permute-start | bytes 1572872 | tf_op jit(solution)/shard_map/ppermute | solution.py:435
  48.3 28.4 %collective-permute-start.11 = (bf16[512,512]{1,0:T(8,128)(2,1)S(1)}, bf16[512,512]{1,0:T(8,128)(2,1)}, u32[]{:S(2)}, u32[]{:S(2)}) collective-permute-start(bf16[512,512]{1,0:T(8,128)(2,1)S(1)} %collective-permute-done.10.refs_15_), channel_id=1, source_target_pairs={{0,4},{4,0},{8,12},{12,8},{16,20},{20,16},{24,28},{28,24},{1,5},{5... | collective-permute-start | bytes 1572872 | tf_op jit(solution)/shard_map/ppermute | solution.py:435
  52.0 24.7 %collective-permute-start.2 = (bf16[512,512]{1,0:T(8,128)(2,1)}, bf16[512,512]{1,0:T(8,128)(2,1)}, u32[]{:S(2)}, u32[]{:S(2)}) collective-permute-start(bf16[512,512]{1,0:T(8,128)(2,1)} %collective-permute-done.1.refs_5_), channel_id=1, source_target_pairs={{0,4},{4,0},{8,12},{12,8},{16,20},{20,16},{24,28},{28,24},{1,5},{5... | collective-permute-start | bytes 1572872 | tf_op jit(solution)/shard_map/ppermute | solution.py:435
  52.0 24.7 %collective-permute-start.13 = (bf16[512,512]{1,0:T(8,128)(2,1)}, bf16[512,512]{1,0:T(8,128)(2,1)}, u32[]{:S(2)}, u32[]{:S(2)}) collective-permute-start(bf16[512,512]{1,0:T(8,128)(2,1)} %collective-permute-done.12.refs_17_), channel_id=1, source_target_pairs={{0,4},{4,0},{8,12},{12,8},{16,20},{20,16},{24,28},{28,24},{1,5},{5... | collective-permute-start | bytes 1572872 | tf_op jit(solution)/shard_map/ppermute | solution.py:435
  59.1 17.6 %collective-permute-start.6 = (bf16[512,512]{1,0:T(8,128)(2,1)}, bf16[512,512]{1,0:T(8,128)(2,1)}, u32[]{:S(2)}, u32[]{:S(2)}) collective-permute-start(bf16[512,512]{1,0:T(8,128)(2,1)} %collective-permute-done.5.refs_9_), channel_id=1, source_target_pairs={{0,4},{4,0},{8,12},{12,8},{16,20},{20,16},{24,28},{28,24},{1,5},{5... | collective-permute-start | bytes 1572872 | tf_op jit(solution)/shard_map/ppermute | solution.py:435
  112.0 7.5 %collective-permute-start.23 = (bf16[128,1024]{1,0:T(8,128)(2,1)S(1)}, bf16[128,1024]{1,0:T(8,128)(2,1)S(1)}, u32[]{:S(2)}, u32[]{:S(2)}) collective-permute-start(bf16[128,1024]{1,0:T(8,128)(2,1)S(1)} %pad_maximum_fusion.1), channel_id=1, source_target_pairs={{0,8},{4,12},{8,0},{12,4},{16,24},{20,28},{24,16},{28,20},{1,9},{5... | collective-permute-start | bytes 786440 | tf_op jit(solution)/shard_map/ppermute | solution.py:435
  113.6 17.6 %collective-permute-start.26 = (bf16[4,128,1024]{2,1,0:T(8,128)(2,1)}, bf16[4,128,1024]{2,1,0:T(8,128)(2,1)}, u32[]{:S(2)}, u32[]{:S(2)}) collective-permute-start(bf16[4,128,1024]{2,1,0:T(8,128)(2,1)} %get-tuple-element.43), channel_id=1, source_target_pairs={{0,4},{4,0},{8,12},{12,8},{16,20},{20,16},{24,28},{28,24},{1,5},{5... | collective-permute-start | bytes 3145736 | tf_op jit(solution)/shard_map/ppermute | solution.py:435
  131.1 102.2 %reduce-scatter.7.cloned.1.call-start = ((), (), s32[]{:S(2)}) async-start(), calls=%async_computation.6 | async-start | bytes 1310720 | tf_op jit(solution)/shard_map/reduce_scatter | solution.py:502
  140.9 16.5 %collective-permute-start.31 = (bf16[4,128,1024]{2,1,0:T(8,128)(2,1)}, bf16[4,128,1024]{2,1,0:T(8,128)(2,1)}, u32[]{:S(2)}, u32[]{:S(2)}) collective-permute-start(bf16[4,128,1024]{2,1,0:T(8,128)(2,1)} %get-tuple-element.46), channel_id=1, source_target_pairs={{0,4},{4,0},{8,12},{12,8},{16,20},{20,16},{24,28},{28,24},{1,5},{5... | collective-permute-start | bytes 3145736 | tf_op jit(solution)/shard_map/ppermute | solution.py:435
  157.3 76.0 %reduce-scatter.9.cloned.1.call-start = ((), (), s32[]{:S(2)}) async-start(), calls=%async_computation.7 | async-start | bytes 1310720 | tf_op jit(solution)/shard_map/reduce_scatter | solution.py:502
  168.5 16.6 %collective-permute-start.36 = (bf16[4,128,1024]{2,1,0:T(8,128)(2,1)}, bf16[4,128,1024]{2,1,0:T(8,128)(2,1)}, u32[]{:S(2)}, u32[]{:S(2)}) collective-permute-start(bf16[4,128,1024]{2,1,0:T(8,128)(2,1)} %get-tuple-element.49), channel_id=1, source_target_pairs={{0,4},{4,0},{8,12},{12,8},{16,20},{20,16},{24,28},{28,24},{1,5},{5... | collective-permute-start | bytes 3145736 | tf_op jit(solution)/shard_map/ppermute | solution.py:435
  185.0 58.9 %reduce-scatter.11.cloned.1.call-start = ((), (), s32[]{:S(2)}) async-start(), calls=%async_computation.8 | async-start | bytes 1310720 | tf_op jit(solution)/shard_map/reduce_scatter | solution.py:502
  (33 other events, 314.0 us)
Sparse Core Ops, SparseCore 0:
  131.3 27.3 reduce-scatter.4
  161.1 25.8 reduce-scatter.6
  189.2 25.7 reduce-scatter.8
  217.9 25.9 reduce-scatter.10

commit v2 on v1

v2 whole, which is shorter than its diff:
```python
import functools
import math

import jax
import jax.numpy as jnp
from jax import lax
from jax.experimental import pallas as pl
from jax.experimental.pallas import tpu as pltpu
from jax.sharding import PartitionSpec as P

DH = 128
BLK = 128
MAXL = 2
HIGH = lax.Precision.HIGHEST
F32 = jnp.float32
BF16 = jnp.bfloat16
VMEM_BYTES = 60 * 1024 * 1024


def nn(a, b):
    return lax.dot_general(a, b, (((1,), (0,)), ((), ())), preferred_element_type=F32)


def nt(a, b):
    return lax.dot_general(a, b, (((1,), (1,)), ((), ())), preferred_element_type=F32)


def tn(a, b):
    return lax.dot_general(a, b, (((0,), (0,)), ((), ())), preferred_element_type=F32)


def nn_high(a, b):
    return lax.dot_general(
        a, b, (((1,), (0,)), ((), ())), precision=HIGH, preferred_element_type=F32
    )


def nt_high(a, b):
    return lax.dot_general(
        a, b, (((1,), (1,)), ((), ())), precision=HIGH, preferred_element_type=F32
    )


def split(value):
    top = value.astype(BF16)
    return top, (value - top.astype(F32)).astype(BF16)


def iota(shape, dim):
    return lax.broadcasted_iota(jnp.int32, shape, dim)


def head(h):
    return slice(h * DH, (h + 1) * DH)


def listed(ints_ref, entry, entries):
    return ints_ref[1 + entry], ints_ref[1 + entries + entry]


def compiler_params():
    return pltpu.CompilerParams(vmem_limit_bytes=VMEM_BYTES)


def cost(microseconds):
    return pl.CostEstimate(
        flops=int(microseconds * 1.15e9), bytes_accessed=1 << 20, transcendentals=0
    )


def in_smem(count):
    return [pl.BlockSpec(memory_space=pltpu.SMEM)] * count


def in_vmem(count):
    return [pl.BlockSpec(memory_space=pltpu.VMEM)] * count


def chain_kernel(heads, house_ref, unit_ref, rows_ref, inv_ref, unit_t_ref, unit_h):
    count = house_ref.shape[0]
    eye = (iota((count, count), 0) == iota((count, count), 1)).astype(F32)
    for h in range(heads):
        house = house_ref[:, head(h)]
        lengths = jnp.sqrt(jnp.sum(house * house, axis=1, keepdims=True) + 1e-06)
        unit_ref[:, head(h)] = house / lengths
        unit_h[h] = house / lengths
        inv_ref[h] = eye

    def eliminate(step, carry):
        below = iota((count, 1), 0) > step
        for h in range(heads):
            pivot = unit_h[h, pl.ds(step, 1), :]
            overlap = jnp.sum(unit_h[h] * pivot, axis=1, keepdims=True)
            factor = jnp.where(below, 2.0 * overlap, 0.0)
            inv_ref[h] = inv_ref[h] - factor * inv_ref[h, pl.ds(step, 1), :]
        return carry

    lax.fori_loop(0, count, eliminate, 0)
    eye_wide = (iota((DH, DH), 0) == iota((DH, DH), 1)).astype(F32)
    for h in range(heads):
        units = unit_ref[:, head(h)]
        rows_ref[:, head(h)] = nn_high(inv_ref[h], units)
        unit_t_ref[h] = nt_high(eye_wide, units)


def run_chain(house_all, heads):
    count, width = house_all.shape
    return pl.pallas_call(
        functools.partial(chain_kernel, heads),
        out_shape=[
            jax.ShapeDtypeStruct((count, width), F32),
            jax.ShapeDtypeStruct((count, width), F32),
            jax.ShapeDtypeStruct((heads, count, count), F32),
            jax.ShapeDtypeStruct((heads, DH, count), F32),
        ],
        in_specs=in_vmem(1),
        out_specs=in_vmem(4),
        scratch_shapes=[pltpu.VMEM((heads, count, DH), F32)],
        compiler_params=compiler_params(),
        cost_estimate=cost(6),
        name="house_chain",
    )(house_all)


def rotate_kernel(
    heads,
    blocks,
    ints_ref,
    after_ref,
    rows_ref,
    unit_t_ref,
    query_ref,
    key_ref,
    qrot_ref,
    krot_ref,
    local_ref,
    list_hi_ref,
    list_lo_ref,
):
    count = rows_ref.shape[0]
    entries = blocks * MAXL
    eye = (iota((DH, DH), 0) == iota((DH, DH), 1)).astype(F32)

    def cumulative(h, block):
        kept = jnp.where(iota((DH, count), 1) <= block, unit_t_ref[h], 0.0)
        return split(eye - 2.0 * nn_high(kept, rows_ref[:, head(h)]))

    base = ints_ref[0] * blocks

    def local_block(b, carry):
        here = pl.ds(pl.multiple_of(b * BLK, BLK), BLK)
        for h in range(heads):
            hi, lo = cumulative(h, base + b)
            local_ref[b, h] = hi
            query, key = query_ref[here, head(h)], key_ref[here, head(h)]
            qrot_ref[here, head(h)] = (nn(query, hi) + nn(query, lo)).astype(BF16)
            krot_ref[here, head(h)] = (nn(key, hi) + nn(key, lo)).astype(BF16)
        return carry

    lax.fori_loop(0, blocks, local_block, 0)

    def listed_block(e, carry):
        owner, offset = listed(ints_ref, e, entries)
        for h in range(heads):
            hi, lo = cumulative(h, owner * blocks + offset)
            list_hi_ref[e, h] = hi
            list_lo_ref[e, h] = lo
        return carry

    lax.fori_loop(0, entries, listed_block, 0)


def run_rotate(ints, after, house_rows, unit_t, query_rows, key_rows, heads, blocks):
    rows, width = query_rows.shape
    entries = blocks * MAXL
    return pl.pallas_call(
        functools.partial(rotate_kernel, heads, blocks),
        out_shape=[
            jax.ShapeDtypeStruct((rows, width), BF16),
            jax.ShapeDtypeStruct((rows, width), BF16),
            jax.ShapeDtypeStruct((blocks, heads, DH, DH), BF16),
            jax.ShapeDtypeStruct((entries, heads, DH, DH), BF16),
            jax.ShapeDtypeStruct((entries, heads, DH, DH), BF16),
        ],
        in_specs=in_smem(1) + [pl.BlockSpec(memory_space=pl.ANY)] + in_vmem(4),
        out_specs=in_vmem(5),
        compiler_params=compiler_params(),
        cost_estimate=cost(9),
        name="rotate",
    )(ints, after, house_rows, unit_t, query_rows, key_rows)


def attend_kernel(heads, blocks, places, pieces, *refs):
    ints_ref = refs[0]
    source_count = 1 + max(place[0] for pair in places for place in pair)
    sources = refs[1 : 1 + source_count]
    refs = refs[1 + source_count :]
    (query_ref, qrot_ref, krot_ref, value_ref, grad_ref, local_ref, hi_ref, lo_ref) = refs[:8]
    dq_ref, dcum_ref, dk_ref, dv_ref = refs[8:12]
    outs = refs[12 : 12 + max(pieces, 1)]
    refs = refs[12 + max(pieces, 1) :]
    far_keys, far_values, sems = refs[:3]
    entries = blocks * MAXL
    scaling = DH ** (-0.5)
    log_scale = scaling * math.log2(math.e)

    def start(e, src, kind, slot, where):
        pltpu.make_async_copy(src.at[where], slot.at[e], sems.at[kind, e]).start()

    for e in range(entries):
        owner, offset = listed(ints_ref, e, entries)
        row = pl.multiple_of(offset * BLK, BLK)
        if len(places) == 1:
            start(e, sources[0], 0, far_keys, (owner, pl.ds(row, BLK)))
            start(e, sources[1], 1, far_values, (owner, pl.ds(row, BLK)))
        else:
            distance = owner ^ ints_ref[0]
            for r, (key_place, value_place) in enumerate(places):

                @pl.when(distance == r)
                def _():
                    source, first = key_place
                    start(e, sources[source], 0, far_keys, pl.ds(first + row, BLK))
                    source, first = value_place
                    start(e, sources[source], 1, far_values, pl.ds(first + row, BLK))

    out_copies = []
    if pieces:
        payloads, out_sems = refs[3 : 3 + heads], refs[3 + heads]
        for payload in payloads:
            payload[...] = jnp.zeros_like(payload)
    for kind, slots in ((0, far_keys), (1, far_values)):
        for e in range(entries):
            pltpu.make_async_copy(slots.at[e], slots.at[e], sems.at[kind, e]).wait()

    later = iota((BLK, BLK), 0) > iota((BLK, BLK), 1)
    for h in range(heads):
        lanes = head(h)
        for a in range(blocks):
            here = slice(a * BLK, (a + 1) * BLK)
            qrot, grad = qrot_ref[here, lanes], grad_ref[here, lanes]
            keys = [krot_ref[b * BLK : (b + 1) * BLK, lanes] for b in range(a + 1)]
            values = [value_ref[b * BLK : (b + 1) * BLK, lanes] for b in range(a + 1)]
            for l in range(MAXL):
                e = a * MAXL + l
                raw = far_keys[e, :, lanes]
                keys.append((nn(raw, hi_ref[e, h]) + nn(raw, lo_ref[e, h])).astype(BF16))
                values.append(far_values[e, :, lanes])
            scores, top = [], None
            for b, key in enumerate(keys):
                part = nt(key, qrot) * log_scale
                if b == a:
                    part = jnp.where(later, -jnp.inf, part)
                scores.append(part)
                top = part if top is None else jnp.maximum(top, part)
            top = jnp.max(top, axis=0, keepdims=True)
            weights, dprobs, total, inner = [], [], None, None
            for part, value in zip(scores, values):
                weight = jnp.exp2(part - top)
                dprob = nt(value, grad)
                weights.append(weight)
                dprobs.append(dprob)
                product = weight * dprob
                total = weight if total is None else total + weight
                inner = product if inner is None else inner + product
            inverse = 1.0 / jnp.sum(total, axis=0, keepdims=True)
            delta = jnp.sum(inner, axis=0, keepdims=True) * inverse
            dscores = []
            for b in range(a + 1 + MAXL):
                probs = weights[b] * inverse
                probs_b = probs.astype(BF16)
                dscore = (probs * (dprobs[b] - delta)).astype(BF16)
                dscores.append(dscore)
                dkey, dvalue = nn(dscore, qrot) * scaling, nn(probs_b, grad)
                spot = slice(b * BLK, (b + 1) * BLK)
                if b < a:
                    dk_ref[spot, lanes] += dkey
                    dv_ref[spot, lanes] += dvalue
                elif b == a:
                    dk_ref[spot, lanes] = dkey
                    dv_ref[spot, lanes] = dvalue
                else:
                    e = a * MAXL + b - a - 1
                    dkey, dvalue = dkey.astype(BF16), dvalue.astype(BF16)
                    if pieces:
                        owner, offset = listed(ints_ref, e, entries)
                        distance = owner ^ ints_ref[0]
                        at = (distance & 1) * blocks + offset
                        payloads[h][at, distance >> 1, :, :DH] += dkey
                        payloads[h][at, distance >> 1, :, DH:] += dvalue
                    else:
                        outs[0][e, :, 2 * h * DH : (2 * h + 1) * DH] = dkey
                        outs[0][e, :, (2 * h + 1) * DH : (2 * h + 2) * DH] = dvalue
            dscores, keys = jnp.concatenate(dscores, axis=0), jnp.concatenate(keys, axis=0)
            dq_top, dq_low = split(tn(dscores, keys) * scaling)
            dq_ref[here, lanes] = nt(dq_top, local_ref[a, h]).astype(BF16)
            query = query_ref[here, lanes]
            dcum_ref[a, h] = tn(query, dq_top) + tn(query, dq_low)
        for i in range(pieces):
            where = outs[i].at[:, :, 2 * h * DH : (2 * h + 2) * DH]
            copy = pltpu.make_async_copy(payloads[h].at[i], where, out_sems.at[i, h])
            copy.start()
            out_copies.append(copy)
    for copy in out_copies:
        copy.wait()


def run_attend(ints, sources, places, arrays, heads, blocks, pieces):
    rows, width = arrays[0].shape
    entries = blocks * MAXL
    any_spec = pl.BlockSpec(memory_space=pl.ANY)
    scratch = [
        pltpu.VMEM((entries, BLK, width), BF16),
        pltpu.VMEM((entries, BLK, width), BF16),
        pltpu.SemaphoreType.DMA((2, entries)),
    ]
    if pieces:
        chips = len(places) // 2
        out_parts = [jax.ShapeDtypeStruct((chips, BLK, 2 * width), BF16)] * pieces
        part_specs = [any_spec] * pieces
        scratch += [pltpu.VMEM((pieces, chips, BLK, 2 * DH), BF16)] * heads
        scratch += [pltpu.SemaphoreType.DMA((pieces, heads))]
    else:
        out_parts = [jax.ShapeDtypeStruct((entries, BLK, 2 * width), BF16)]
        part_specs = in_vmem(1)
    return pl.pallas_call(
        functools.partial(attend_kernel, heads, blocks, places, pieces),
        out_shape=[
            jax.ShapeDtypeStruct((rows, width), BF16),
            jax.ShapeDtypeStruct((blocks, heads, DH, DH), F32),
            jax.ShapeDtypeStruct((rows, width), F32),
            jax.ShapeDtypeStruct((rows, width), F32),
        ]
        + out_parts,
        in_specs=in_smem(1) + [any_spec] * len(sources) + in_vmem(8),
        out_specs=in_vmem(4) + part_specs,
        scratch_shapes=scratch,
        compiler_params=compiler_params(),
        cost_estimate=cost(15),
        name="attend",
    )(ints, *sources, *arrays)


def merge_kernel(own_ref, got_ref, after_ref, *out_refs):
    for i, ref in enumerate(out_refs):
        total = own_ref[i + 1].astype(F32) + got_ref[i + 1].astype(F32)
        ref[...] = total.astype(BF16)


def run_merge(own, got, after):
    chips, rows, width = own.shape
    return pl.pallas_call(
        merge_kernel,
        out_shape=[jax.ShapeDtypeStruct((rows, width), BF16)] * (chips - 1),
        in_specs=in_vmem(2) + [pl.BlockSpec(memory_space=pl.ANY)],
        out_specs=in_vmem(chips - 1),
        compiler_params=compiler_params(),
        cost_estimate=cost(1.5),
        name="merge",
    )(own, got, after)


def project_kernel(heads, parts, per, flip_ref, *refs):
    part_refs = refs[:parts]
    dk_loc, dv_loc, dq_ref, key_ref, dcum_in, cum_ref, wq, wk, wv = refs[parts : parts + 9]
    first_ref, rest_ref, dcum_out, dk_ref, dv_ref = refs[parts + 9 :]
    step = pl.program_id(0)

    @pl.when(step == 0)
    def _():
        for h in range(heads):
            both = slice(2 * h * DH, (2 * h + 2) * DH)
            total = part_refs[0][0, :, both].astype(F32)
            for ref in part_refs[1:]:
                total = total + ref[0, :, both].astype(F32)
            dv_ref[:, head(h)] = (dv_loc[:, head(h)] + total[:, DH:]).astype(BF16)
            dk_top, dk_low = split(dk_loc[:, head(h)] + total[:, :DH])
            dk_ref[:, head(h)] = nt(dk_top, cum_ref[0, h]).astype(BF16)
            key = key_ref[:, head(h)]
            dcum_out[h] = dcum_in[0, h] + tn(key, dk_top) + tn(key, dk_low)

    term = nt(wq[...], dq_ref[...]) + nt(wk[...], dk_ref[...]) + nt(wv[...], dv_ref[...])
    term = term.T.astype(BF16)

    @pl.when(step < per)
    def _():
        first_ref[...] = term

    @pl.when(step >= per)
    def _():
        rest_ref[0] = term


def run_project(block, flip, parts, dk_loc, dv_loc, dq, key_rows, dcum, cum, weights, groups):
    width = dq.shape[1]
    heads = width // DH
    model = weights[0].shape[0]
    chunk = model // groups
    tile = min(512, chunk)
    per = chunk // tile

    def weight_tile(t, flip):
        m = t // per
        return (m + flip[0] * (groups - 1 - 2 * m)) * per + t % per, 0

    def rest_tile(t, flip):
        later = jnp.maximum(t - per, 0)
        return later // per, 0, later % per

    rows_spec = pl.BlockSpec((BLK, width), lambda t, flip: (block, 0))
    part_spec = pl.BlockSpec((1, BLK, 2 * width), lambda t, flip: (0, 0, 0))
    head_spec = pl.BlockSpec((1, heads, DH, DH), lambda t, flip: (block, 0, 0, 0))
    weight_spec = pl.BlockSpec((tile, width), weight_tile)
    return pl.pallas_call(
        functools.partial(project_kernel, heads, len(parts), per),
        grid_spec=pltpu.PrefetchScalarGridSpec(
            num_scalar_prefetch=1,
            grid=(model // tile,),
            in_specs=[part_spec] * len(parts)
            + [rows_spec] * 4
            + [head_spec] * 2
            + [weight_spec] * 3,
            out_specs=[
                pl.BlockSpec((BLK, tile), lambda t, flip: (0, jnp.minimum(t, per - 1))),
                pl.BlockSpec((1, BLK, tile), rest_tile),
                pl.BlockSpec((heads, DH, DH), lambda t, flip: (0, 0, 0)),
            ],
            scratch_shapes=[pltpu.VMEM((BLK, width), BF16), pltpu.VMEM((BLK, width), BF16)],
        ),
        out_shape=[
            jax.ShapeDtypeStruct((BLK, chunk), BF16),
            jax.ShapeDtypeStruct((groups - 1, BLK, chunk), BF16),
            jax.ShapeDtypeStruct((heads, DH, DH), F32),
        ],
        compiler_params=compiler_params(),
        cost_estimate=cost(5),
        name="project",
    )(flip, *parts, dk_loc, dv_loc, dq, key_rows, dcum, cum, *weights)


def adjoint_kernel(heads, blocks, base_ref, after_ref, *refs):
    dcums = refs[:blocks]
    unit_ref, rows_ref, inv_ref, out_ref = refs[blocks:]
    count, width = unit_ref.shape
    square = (count, count)
    eye = (iota(square, 0) == iota(square, 1)).astype(F32)
    row, col = iota(square, 0), iota(square, 1)
    for h in range(heads):
        units, rows, inverse = unit_ref[:, head(h)], rows_ref[:, head(h)], inv_ref[h]
        inverse_t = nt_high(eye, inverse)
        x_total = jnp.zeros((count, DH), F32)
        y_total = jnp.zeros((count, DH), F32)
        for j in range(blocks):
            mine = base_ref[0] * blocks + j
            dcum = dcums[j][h]
            live = iota((count, 1), 0) <= mine
            moved = nt_high(rows, dcum)
            overlap = jnp.where(col <= mine, nt_high(moved, units), 0.0)
            gamma = nn_high(overlap, inverse)
            gamma = jnp.where((row < col) & (col <= mine), gamma, 0.0)
            x_total += jnp.where(live, moved - 2.0 * nn_high(gamma, units), 0.0)
            beta = jnp.where(col <= mine, eye - inverse_t, 0.0)
            turned = jnp.where(live, units - nn_high(beta, units), 0.0)
            y_total += nn_high(turned, dcum)
        out_ref[:, head(h)] = x_total
        out_ref[:, slice(width + h * DH, width + (h + 1) * DH)] = y_total


def run_adjoint(ints, after, dcums, unit, rows, inverse, heads, blocks):
    count, width = unit.shape
    return pl.pallas_call(
        functools.partial(adjoint_kernel, heads, blocks),
        out_shape=jax.ShapeDtypeStruct((count, 2 * width), F32),
        in_specs=in_smem(1) + [pl.BlockSpec(memory_space=pl.ANY)] + in_vmem(blocks + 3),
        out_specs=pl.BlockSpec(memory_space=pltpu.VMEM),
        compiler_params=compiler_params(),
        cost_estimate=cost(11),
        name="adjoint",
    )(ints, after, *dcums, unit, rows, inverse)


def house_kernel(heads, blocks, base_ref, got_ref, unit_ref, rows_ref, house_ref, out_ref):
    count, width = unit_ref.shape
    total = jnp.sum(got_ref[...], axis=0)
    for h in range(heads):
        x_part = total[:, head(h)]
        y_part = total[:, slice(width + h * DH, width + (h + 1) * DH)]
        along = nt_high(y_part, rows_ref[:, head(h)])
        spot = iota((blocks, count), 0) + base_ref[0] * blocks
        along = jnp.where(iota((blocks, count), 1) < spot, along, 0.0)
        turned = y_part - 2.0 * nn_high(along, unit_ref[:, head(h)])
        dunit = -2.0 * (x_part + turned)
        house = house_ref[:, head(h)]
        lengths = jnp.sqrt(jnp.sum(house * house, axis=1, keepdims=True) + 1e-06)
        unit = house / lengths
        inner = jnp.sum(unit * dunit, axis=1, keepdims=True)
        out_ref[:, head(h)] = (dunit - unit * inner) / lengths


def run_house(ints, got, unit, rows, house_dirs, heads, blocks):
    return pl.pallas_call(
        functools.partial(house_kernel, heads, blocks),
        out_shape=jax.ShapeDtypeStruct(house_dirs.shape, F32),
        in_specs=[pl.BlockSpec(memory_space=pltpu.SMEM)] + in_vmem(4),
        out_specs=pl.BlockSpec(memory_space=pltpu.VMEM),
        compiler_params=compiler_params(),
        cost_estimate=cost(2),
        name="house_grad",
    )(ints, got, unit, rows, house_dirs)


def hop(value, distance, count):
    return lax.ppermute(value, "ctx", [(i, i ^ distance) for i in range(count)])


def slide(value, pairs):
    return lax.ppermute(value, "head", pairs)


def line_scatter(first, rest):
    place = lax.axis_index("head")
    ends = (place == 0) | (place == 3)
    inward = slide(rest, [(0, 1), (3, 2)])
    swapped = slide(rest[1:] + inward[1:], [(1, 2), (2, 1)])
    outward = slide(first + swapped[1], [(1, 0), (2, 3)])
    total = jnp.where(ends, first, rest[0]).astype(F32) + inward[0].astype(F32)
    total = total + swapped[0].astype(F32) + outward.astype(F32)
    return total.astype(BF16), inward


def shards(
    query_rows, key_rows, value_rows, grad_out, house_dirs, owners, offsets, w_query, w_key, w_value
):
    tok_rows, width = query_rows.shape
    heads, blocks = width // DH, tok_rows // BLK
    ctx_count, groups = lax.axis_size("ctx"), lax.axis_size("head")
    my_index = lax.axis_index("ctx").astype(jnp.int32)
    ints = jnp.concatenate([my_index.reshape(1), owners.reshape(-1), offsets.reshape(-1)])
    by_hand = ctx_count == 8
    core, across, along = 1, 2, 4

    if by_hand:
        house_all = house_dirs
        for distance in (core, across, along):
            other = hop(house_all, distance, 8)
            upper = (my_index & distance) != 0
            low, high = jnp.where(upper, other, house_all), jnp.where(upper, house_all, other)
            house_all = jnp.concatenate([low, high], axis=0)
        both = jnp.concatenate([key_rows, value_rows], axis=0)
        both_s, both_x, both_y = hop(both, core, 8), hop(both, across, 8), hop(both, along, 8)
        key_d, value_d = hop(both_y[:tok_rows], across, 8), hop(both_x[tok_rows:], along, 8)
        both_xs, both_ys = hop(both_x, core, 8), hop(both_y, core, 8)
        key_ds, value_ds = hop(key_d, core, 8), hop(value_d, core, 8)
        sources = [key_rows, value_rows, both_s, both_x, both_xs, both_y, both_ys]
        sources += [key_d, value_d, key_ds, value_ds]
        places = [((0, 0), (1, 0))] + [((i, 0), (i, tok_rows)) for i in range(2, 7)]
        places += [((7, 0), (8, 0)), ((9, 0), (10, 0))]
        after = both_x
    else:
        house_all = lax.all_gather(house_dirs, "ctx", axis=0, tiled=True)
        sources = [lax.all_gather(key_rows, "ctx"), lax.all_gather(value_rows, "ctx")]
        places = [((0, 0), (1, 0))]
        after = key_rows

    unit, rows, inverse, unit_t = run_chain(house_all, heads)
    qrot, krot, local, list_hi, list_lo = run_rotate(
        ints, after, rows, unit_t, query_rows, key_rows, heads, blocks
    )
    pieces = 2 * blocks if by_hand else 0
    dq, dcum, dk_loc, dv_loc, *outs = run_attend(
        ints,
        sources,
        places,
        (query_rows, qrot, krot, value_rows, grad_out, local, list_hi, list_lo),
        heads,
        blocks,
        pieces,
    )
    if not by_hand:
        spots = (owners * blocks + offsets).reshape(-1)
        empty = jnp.zeros((ctx_count * blocks, BLK, 2 * width), BF16)
        filled = empty.at[spots].add(outs[0])
        back = lax.psum_scatter(filled, "ctx", scatter_dimension=0, tiled=True)

    weights = (w_query, w_key, w_value)
    on_line = groups == 4
    flip = jnp.where(on_line & (lax.axis_index("head") >= 2), 1, 0).astype(jnp.int32).reshape(1)
    share = jnp.zeros((tok_rows, w_query.shape[0] // groups), BF16)
    dcums, after = [], key_rows
    for j in range(blocks):
        if by_hand:
            got = hop(outs[blocks + j], core, 8)
            to_x, to_y, to_d = run_merge(outs[j], got, after)
            parts = [outs[j], got, hop(to_x, across, 8)[None], hop(to_y, along, 8)[None]]
            after = hop(to_d, across + along, 8)
            parts.append(after[None])
        else:
            parts = [back[j : j + 1]]
        first, rest, dcum_j = run_project(
            j, flip, parts, dk_loc, dv_loc, dq, key_rows, dcum, local, weights, groups
        )
        dcums.append(dcum_j)
        if on_line:
            done, inward = line_scatter(first, rest)
            late = inward if j < blocks - 1 else late
        else:
            late = rest
            term = jnp.concatenate([first[None], rest], axis=0)
            done = lax.psum_scatter(term, "head", scatter_dimension=0, tiled=False)
        share = lax.dynamic_update_slice(share, done, (j * BLK, 0))

    sums = run_adjoint(ints, late, dcums, unit, rows, inverse, heads, blocks)
    sums = sums.reshape(ctx_count, blocks, 2 * width)
    got = lax.all_to_all(sums, "ctx", split_axis=0, concat_axis=0, tiled=True)
    house_grad = run_house(ints, got, unit, rows, house_dirs, heads, blocks)
    return (share, house_grad)


def solution(mesh):
    placed = (
        P("ctx", "head"),
        P("ctx", "head"),
        P("ctx", "head"),
        P("ctx", "head"),
        P("ctx", "head"),
        P("ctx", None),
        P("ctx", None),
        P(None, "head"),
        P(None, "head"),
        P(None, "head"),
    )
    return jax.shard_map(
        shards,
        mesh=mesh,
        in_specs=placed,
        out_specs=(P("ctx", "head"), P("ctx", "head")),
        check_vma=False,
    )
```

time: 254 us -> 250 us (0.984)
  waiting for transfers between devices: 89.7 us -> 59.1 us
  starting transfers between devices: 32.2 us -> 49.9 us
  Pallas kernels: 93 us -> 109 us
  between operations: 14.1 us -> 1.09 us
  blocking collectives: 8.01 us -> 0 us
  local copies, waits for them, and re-layouts: 6.63 us -> 13.6 us
  other arithmetic: 8.99 us -> 15 us
    ppermute x41 -> x28, waiting for transfers between devices: 79.1 us -> 35.7 us  [hop(): return lax.ppermute(value, 'ctx', [(i, i ^ distance) for i in range(count)])]
    ppermute x0 -> x12, waiting for transfers between devices: none -> 20.7 us  [slide(): return lax.ppermute(value, 'head', pairs)]
    ppermute x0 -> x12, starting transfers between devices: none -> 20.2 us  [slide(): return lax.ppermute(value, 'head', pairs)]
    pallas_call x6 -> x11, Pallas kernels: 80.3 us -> 93.6 us  [the longest x4 46.4 us: run_project(): pl.pallas_call(functools.partial(project_kernel, heads, len(parts), per),...]
    reduce_scatter x4 -> x0, waiting for transfers between devices: 10.6 us -> none  [shards(): lax.psum_scatter(term, 'head', scatter_dimension=0, tiled=False)]
    all_to_all x1 -> x0, blocking collectives: 8.01 us -> none  [shards(): got = lax.all_to_all(sums, 'ctx', split_axis=0, concat_axis=0, tiled=True)]
    ppermute x41 -> x28, starting transfers between devices: 32.1 us -> 26.4 us  [hop(): return lax.ppermute(value, 'ctx', [(i, i ^ distance) for i in range(count)])]
    unnamed x33 -> x61, local copies, waits for them, and re-layouts: 5.72 us -> 9.83 us
  transfers between devices with their start and end apart: 45 -> 41, of which waited for: 24 -> 10; matrix products, arithmetic and copies ran while one was open for 3% -> 8% of each run, Pallas kernels for 28% -> 36%
where the time goes in v2:
time: 250 us; the launch traced here: 248 us
  Pallas kernels  109 us (44%)
  waiting for transfers between devices  59.1 us (24%)
  starting transfers between devices  49.9 us (20%)
  other arithmetic  15 us (6%)
  local copies, waits for them, and re-layouts  13.6 us (5%)
    pallas_call x4, Pallas kernels, run_project(): pl.pallas_call(functools.partial(project_kernel, heads, len(parts), per),...  46.4 us
    ppermute x28, waiting for transfers between devices, hop(): return lax.ppermute(value, 'ctx', [(i, i ^ distance) for i in range(count)])  35.7 us
    ppermute x28, starting transfers between devices, hop(): return lax.ppermute(value, 'ctx', [(i, i ^ distance) for i in range(count)])  26.4 us
    pallas_call x1, Pallas kernels, run_attend(): pl.pallas_call(functools.partial(attend_kernel, heads, blocks, places, pi...  20.9 us
    ppermute x12, waiting for transfers between devices, slide(): return lax.ppermute(value, 'head', pairs)  20.7 us
    ppermute x12, starting transfers between devices, slide(): return lax.ppermute(value, 'head', pairs)  20.2 us
    pallas_call x1, Pallas kernels, run_adjoint(): pl.pallas_call(functools.partial(adjoint_kernel, heads, blocks), out_shap...  13 us
    pallas_call x1, Pallas kernels, run_rotate(): pl.pallas_call(functools.partial(rotate_kernel, heads, blocks), out_shape...  10.9 us
  transfers between devices with their start and end apart: 41, of which 10 were waited for; matrix products, arithmetic and copies ran while one was open for 8% of the time, Pallas kernels for 36%

profile of v2, /device:TPU:0, one launch (start us, length us, event | category | flops | bytes accessed | tf_op | source)
XLA Modules:
  0.0 247.9 jit_solution(17393934372242329069)
XLA Ops:
  4.9 2.5 %collective-permute-start.1 = (bf16[1024,512]{1,0:T(8,128)(2,1)}, bf16[1024,512]{1,0:T(8,128)(2,1)S(1)}, u32[]{:S(2)}, u32[]{:S(2)}) collective-permute-start(bf16[1024,512]{1,0:T(8,128)(2,1)} %constant_dynamic-update-slice_fusion), channel_id=1, source_target_pairs={{0,8},{4,12},{8,0},{12,4},{16,24},{20,28},{24,16},{28,20},{1,9},{5... | collective-permute-start | bytes 3145736 | tf_op jit(solution)/shard_map/ppermute | solution.py:513
  11.9 19.8 %collective-permute-done.10 = f32[8,512]{1,0:T(8,128)S(1)} collective-permute-done((f32[8,512]{1,0:T(8,128)S(1)}, f32[8,512]{1,0:T(8,128)S(1)}, u32[]{:S(2)}, u32[]{:S(2)}) %collective-permute-start.10) | collective-permute-done | bytes 16416 | tf_op jit(solution)/shard_map/ppermute | solution.py:513
  40.4 5.4 %house_chain.1 = (f32[32,512]{1,0:T(8,128)}, f32[32,512]{1,0:T(8,128)}, f32[4,32,32]{2,1,0:T(8,128)}, f32[4,128,32]{2,1,0:T(8,128)}) custom-call(f32[32,512]{1,0:T(8,128)} %pad_maximum_fusion.house_ref), custom_call_target="tpu_custom_call" | custom-call | flops 6899999744 | bytes 1048576 | tf_op jit(solution)/shard_map/house_chain/pallas_call | solution.py:108
  45.8 3.3 %collective-permute-done.6.refs_9_ = bf16[512,512]{1,0:T(8,128)(2,1)S(1)} collective-permute-done((bf16[512,512]{1,0:T(8,128)(2,1)S(1)}, bf16[512,512]{1,0:T(8,128)(2,1)S(1)}, u32[]{:S(2)}, u32[]{:S(2)}) %collective-permute-start.6) | collective-permute-done | bytes 524320 | tf_op jit(solution)/shard_map/ppermute | solution.py:513
  50.6 10.9 %rotate.1 = (bf16[512,512]{1,0:T(8,128)(2,1)}, bf16[512,512]{1,0:T(8,128)(2,1)}, bf16[4,4,128,128]{3,2,1,0:T(8,128)(2,1)}, bf16[8,4,128,128]{3,2,1,0:T(8,128)(2,1)}, bf16[8,4,128,128]{3,2,1,0:T(8,128)(2,1)}) custom-call(s32[17]{0:T(128)} %pad_add_fusion.ints_ref.refs_0_.base_ref, bf16[1024,512]{1,0:T(8,128)(2,1)} %copy-done.9, ...), custom_call_target="tpu_custom_call" | custom-call | flops 10350000128 | bytes 1048576 | tf_op jit(solution)/shard_map/rotate/pallas_call | solution.py:176
  62.5 20.9 %attend.1 = (bf16[512,512]{1,0:T(8,128)(2,1)}, f32[4,4,128,128]{3,2,1,0:T(8,128)}, f32[512,512]{1,0:T(8,128)}, f32[512,512]{1,0:T(8,128)}, bf16[4,128,1024]{2,1,...) custom-call(s32[17]{0:T(128)} %pad_add_fusion.ints_ref.refs_0_.base_, ...), custom_call_target="tpu_custom_call" | custom-call | flops 17250000896 | bytes 1048576 | tf_op jit(solution)/shard_map/attend/pallas_call | solution.py:326
  84.6 2.8 %collective-permute-done.12.got_ref.refs_1_ = bf16[4,128,1024]{2,1,0:T(8,128)(2,1)} collective-permute-done((bf16[4,128,1024]{2,1,0:T(8,128)(2,1)}, bf16[4,128,1024]{2,1,0:T(8,128)(2,1)}, u32[]{:S(2)}, u32[]{:S(2)}) %collective-permute-start.12) | collective-permute-done | bytes 1048608 | tf_op jit(solution)/shard_map/ppermute | solution.py:513
  87.4 2.5 %merge.4 = (bf16[128,1024]{1,0:T(8,128)(2,1)}, bf16[128,1024]{1,0:T(8,128)(2,1)}, bf16[128,1024]{1,0:T(8,128)(2,1)}) custom-call(bf16[4,128,1024]{2,1,0:T(8,128)(2,1)} %get-tuple-element.54.own_ref.refs_0_, bf16[4,128,1024]{2,1,0:T(8,128)(2,1)} %collective-permute-done.12.got_ref.refs_1_, bf16[512,512]{1,0:T(8,128)(2,1)} %refs_8_.7), custom_call_target="tpu_custom_call" | custom-call | flops 1724999936 | bytes 1048576 | tf_op jit(solution)/shard_map/merge/pallas_call | solution.py:352
  93.4 6.8 %collective-permute-done.15.after_ref = bf16[128,1024]{1,0:T(8,128)(2,1)S(1)} collective-permute-done((bf16[128,1024]{1,0:T(8,128)(2,1)}, bf16[128,1024]{1,0:T(8,128)(2,1)S(1)}, u32[]{:S(2)}, u32[]{:S(2)}) %collective-permute-start.15) | collective-permute-done | bytes 262176 | tf_op jit(solution)/shard_map/ppermute | solution.py:513
  107.3 11.5 %project.4 = (bf16[128,1024]{1,0:T(8,128)(2,1)}, bf16[3,128,1024]{2,1,0:T(8,128)(2,1)}, f32[4,128,128]{2,1,0:T(8,128)}) custom-call(s32[1]{0:T(128)} %bitcast.flip_ref, bf16[4,128,1024]{2,1,0:T(8,128)(2,1)} %get-tuple-element.54.own_ref.refs_0_, bf16[4,128,1024]{2,1,0:T(8,128)(2,1)} %collective-permute-done.12.got_ref.refs_1_, ...), custom_call_target="tpu_custom_call" | custom-call | flops 5750000128 | bytes 1048576 | tf_op jit(solution)/shard_map/project/pallas_call | solution.py:414
  118.9 3.7 %collective-permute-start.16 = (bf16[3,128,1024]{2,1,0:T(8,128)(2,1)}, bf16[3,128,1024]{2,1,0:T(8,128)(2,1)S(1)}, u32[]{:S(2)}, u32[]{:S(2)}) collective-permute-start(bf16[3,128,1024]{2,1,0:T(8,128)(2,1)} %get-tuple-element.64), channel_id=1, source_target_pairs={{0,1},{3,2},{4,5},{7,6},{8,9},{11,10},{12,13},{15,14},{16,17},{19,... | collective-permute-start | bytes 2359304 | tf_op jit(solution)/shard_map/ppermute | solution.py:517
  123.3 2.5 %merge.6 = (bf16[128,1024]{1,0:T(8,128)(2,1)}, bf16[128,1024]{1,0:T(8,128)(2,1)}, bf16[128,1024]{1,0:T(8,128)(2,1)}) custom-call(bf16[4,128,1024]{2,1,0:T(8,128)(2,1)} %get-tuple-element.72.own_ref.refs_0_, bf16[4,128,1024]{2,1,0:T(8,128)(2,1)} %copy-done.12, bf16[128,1024]{1,0:T(8,128)(2,1)} %copy-done.19), custom_call_target="tpu_custom_call" | custom-call | flops 1724999936 | bytes 1048576 | tf_op jit(solution)/shard_map/merge/pallas_call | solution.py:352
  129.3 11.6 %project.5 = (bf16[128,1024]{1,0:T(8,128)(2,1)}, bf16[3,128,1024]{2,1,0:T(8,128)(2,1)}, f32[4,128,128]{2,1,0:T(8,128)}) custom-call(s32[1]{0:T(128)} %bitcast.flip_ref, bf16[4,128,1024]{2,1,0:T(8,128)(2,1)} %get-tuple-element.65.own_ref.refs_0_, bf16[4,128,1024]{2,1,0:T(8,128)(2,1)} %copy-done.13, bf16[1,128,1024]{2,1,0:T(8,128)(2,1)} %bitcast.96, ...), custom_call_target="tpu_custom_call" | custom-call | flops 5750000128 | bytes 1048576 | tf_op jit(solution)/shard_map/project/pallas_call | solution.py:414
  143.9 2.5 %merge.7 = (bf16[128,1024]{1,0:T(8,128)(2,1)}, bf16[128,1024]{1,0:T(8,128)(2,1)}, bf16[128,1024]{1,0:T(8,128)(2,1)}) custom-call(bf16[4,128,1024]{2,1,0:T(8,128)(2,1)} %get-tuple-element.79.own_ref.refs_0_, bf16[4,128,1024]{2,1,0:T(8,128)(2,1)} %collective-permute-done.33.got_ref.refs_1_, bf16[128,1024]{1,0:T(8,128)(2,1)} %copy-done.18), custom_call_target="tpu_custom_call" | custom-call | flops 1724999936 | bytes 1048576 | tf_op jit(solution)/shard_map/merge/pallas_call | solution.py:352
  149.9 11.6 %project.6 = (bf16[128,1024]{1,0:T(8,128)(2,1)}, bf16[3,128,1024]{2,1,0:T(8,128)(2,1)}, f32[4,128,128]{2,1,0:T(8,128)}) custom-call(s32[1]{0:T(128)} %bitcast.flip_ref, bf16[4,128,1024]{2,1,0:T(8,128)(2,1)} %get-tuple-element.72.own_ref.refs_0_, bf16[4,128,1024]{2,1,0:T(8,128)(2,1)} %copy-done.12, bf16[1,128,1024]{2,1,0:T(8,128)(2,1)} %bitcast.91, ...), custom_call_target="tpu_custom_call" | custom-call | flops 5750000128 | bytes 1048576 | tf_op jit(solution)/shard_map/project/pallas_call | solution.py:414
  165.3 11.6 %project.7 = (bf16[128,1024]{1,0:T(8,128)(2,1)}, bf16[3,128,1024]{2,1,0:T(8,128)(2,1)}, f32[4,128,128]{2,1,0:T(8,128)}) custom-call(s32[1]{0:T(128)} %bitcast.flip_ref, bf16[4,128,1024]{2,1,0:T(8,128)(2,1)} %get-tuple-element.79.own_ref.refs_0_, bf16[4,128,1024]{2,1,0:T(8,128)(2,1)} %collective-permute-done.33.got_ref.refs_1_, ...), custom_call_target="tpu_custom_call" | custom-call | flops 5750000128 | bytes 1048576 | tf_op jit(solution)/shard_map/project/pallas_call | solution.py:414
  176.9 3.2 %collective-permute-start.37 = (bf16[3,128,1024]{2,1,0:T(8,128)(2,1)}, bf16[3,128,1024]{2,1,0:T(8,128)(2,1)}, u32[]{:S(2)}, u32[]{:S(2)}) collective-permute-start(bf16[3,128,1024]{2,1,0:T(8,128)(2,1)} %get-tuple-element.85), channel_id=1, source_target_pairs={{0,1},{3,2},{4,5},{7,6},{8,9},{11,10},{12,13},{15,14},{16,17},{19,... | collective-permute-start | bytes 2359304 | tf_op jit(solution)/shard_map/ppermute | solution.py:517
  187.4 13.0 %adjoint.1 = f32[32,1024]{1,0:T(8,128)} custom-call(s32[17]{0:T(128)} %pad_add_fusion.ints_ref.refs_0_.base_ref, bf16[3,128,1024]{2,1,0:T(8,128)(2,1)} %copy-done.8, f32[4,128,128]{2,1,0:T(8,128)} %get-tuple-element.86.refs_0_, f32[4,128,128]{2,1,0:T(8,128)} %get-tuple-element.87.refs_1_, f32[4,128,128]{2,1,0:T(8,128)} %get-tuple-element.88.refs_2_, ...), custom_call_target="tpu_custom_call" | custom-call | flops 12650000384 | bytes 1048576 | tf_op jit(solution)/shard_map/adjoint/pallas_call | solution.py:471
  202.0 3.4 %all-to-all-start = ((f32[8,4,1024]{2,1,0:T(4,128)}), f32[8,4,1024]{2,1,0:T(4,128)S(1)}, u32[]{:S(2)}, u32[]{:S(2)}) async-start(f32[8,4,1024]{2,1,0:T(4,128)} %reshape.39), calls=%async_computation | async-start | bytes 262144 | tf_op jit(solution)/shard_map/all_to_all | solution.py:614
  208.2 2.7 %all-to-all-done.got_ref = f32[8,4,1024]{2,1,0:T(4,128)S(1)} async-done(((f32[8,4,1024]{2,1,0:T(4,128)}), f32[8,4,1024]{2,1,0:T(4,128)S(1)}, u32[]{:S(2)}, u32[]{:S(2)}) %all-to-all-start) | async-done | bytes 131104 | tf_op jit(solution)/shard_map/all_to_all | solution.py:614
  211.5 2.6 %house_grad.1 = f32[4,512]{1,0:T(4,128)} custom-call(s32[17]{0:T(128)} %pad_add_fusion.ints_ref.refs_0_.base_ref, f32[8,4,1024]{2,1,0:T(4,128)} %copy-done.11, f32[32,512]{1,0:T(8,128)} %get-tuple-element.90.refs_4_.unit_ref, f32[32,512]{1,0:T(8,128)} %get-tuple-element.47.rows_ref.refs_5_, f32[4,512]{1,0:T(4,128)} %house_ref.1), custom_call_target="tpu_custom_call" | custom-call | flops 2300000000 | bytes 1048576 | tf_op jit(solution)/shard_map/house_grad/pallas_call | solution.py:501
  221.1 4.7 %collective-permute-done.25 = bf16[128,1024]{1,0:T(8,128)(2,1)S(1)} collective-permute-done((bf16[128,1024]{1,0:T(8,128)(2,1)S(1)}, bf16[128,1024]{1,0:T(8,128)(2,1)S(1)}, u32[]{:S(2)}, u32[]{:S(2)}) %collective-permute-start.25) | collective-permute-done | bytes 262176 | tf_op jit(solution)/shard_map/ppermute | solution.py:517
  228.4 6.0 %collective-permute-done.32 = bf16[128,1024]{1,0:T(8,128)(2,1)S(1)} collective-permute-done((bf16[128,1024]{1,0:T(8,128)(2,1)S(1)}, bf16[128,1024]{1,0:T(8,128)(2,1)S(1)}, u32[]{:S(2)}, u32[]{:S(2)}) %collective-permute-start.32) | collective-permute-done | bytes 262176 | tf_op jit(solution)/shard_map/ppermute | solution.py:517
  235.7 10.0 %collective-permute-done.39 = bf16[128,1024]{1,0:T(8,128)(2,1)S(1)} collective-permute-done((bf16[128,1024]{1,0:T(8,128)(2,1)S(1)}, bf16[128,1024]{1,0:T(8,128)(2,1)S(1)}, u32[]{:S(2)}, u32[]{:S(2)}) %collective-permute-start.39) | collective-permute-done | bytes 262176 | tf_op jit(solution)/shard_map/ppermute | solution.py:517
  (158 shorter events, 71.2 us)
Async XLA Ops:
  4.9 31.5 %collective-permute-start.1 = (bf16[1024,512]{1,0:T(8,128)(2,1)}, bf16[1024,512]{1,0:T(8,128)(2,1)S(1)}, u32[]{:S(2)}, u32[]{:S(2)}) collective-permute-start(bf16[1024,512]{1,0:T(8,128)(2,1)} %constant_dynamic-update-slice_fusion), channel_id=1, source_target_pairs={{0,8},{4,12},{8,0},{12,4},{16,24},{20,28},{24,16},{28,20},{1,9},{5... | collective-permute-start | bytes 3145736 | tf_op jit(solution)/shard_map/ppermute | solution.py:513
  7.4 30.9 %collective-permute-start.3 = (bf16[1024,512]{1,0:T(8,128)(2,1)}, bf16[1024,512]{1,0:T(8,128)(2,1)S(1)}, u32[]{:S(2)}, u32[]{:S(2)}) collective-permute-start(bf16[1024,512]{1,0:T(8,128)(2,1)} %constant_dynamic-update-slice_fusion), channel_id=1, source_target_pairs={{0,16},{4,20},{8,24},{12,28},{16,0},{20,4},{24,8},{28,12},{1,17},{... | collective-permute-start | bytes 3145736 | tf_op jit(solution)/shard_map/ppermute | solution.py:513
  9.6 22.1 %collective-permute-start.10 = (f32[8,512]{1,0:T(8,128)S(1)}, f32[8,512]{1,0:T(8,128)S(1)}, u32[]{:S(2)}, u32[]{:S(2)}) collective-permute-start(f32[8,512]{1,0:T(8,128)S(1)} %pad_maximum_fusion.2), channel_id=1, source_target_pairs={{0,8},{4,12},{8,0},{12,4},{16,24},{20,28},{24,16},{28,20},{1,9},{5... | collective-permute-start | bytes 49160 | tf_op jit(solution)/shard_map/ppermute | solution.py:513
  10.2 51.3 %collective-permute-start = (bf16[1024,512]{1,0:T(8,128)(2,1)}, bf16[1024,512]{1,0:T(8,128)(2,1)}, u32[]{:S(2)}, u32[]{:S(2)}) collective-permute-start(bf16[1024,512]{1,0:T(8,128)(2,1)} %constant_dynamic-update-slice_fusion), channel_id=1, source_target_pairs={{0,4},{4,0},{8,12},{12,8},{16,20},{20,16},{24,28},{28,24},{1,5},{5... | collective-permute-start | bytes 3145736 | tf_op jit(solution)/shard_map/ppermute | solution.py:513
  39.9 21.7 %collective-permute-start.2 = (bf16[1024,512]{1,0:T(8,128)(2,1)S(1)}, bf16[1024,512]{1,0:T(8,128)(2,1)}, u32[]{:S(2)}, u32[]{:S(2)}) collective-permute-start(bf16[1024,512]{1,0:T(8,128)(2,1)S(1)} %collective-permute-done.1.after_ref.refs_4_), channel_id=1, source_target_pairs={{0,4},{4,0},{8,12},{12,8},{16,20},{20,16},{24,28},{28,24},{1,5},{5... | collective-permute-start | bytes 3145736 | tf_op jit(solution)/shard_map/ppermute | solution.py:513
  39.9 21.7 %collective-permute-start.4 = (bf16[1024,512]{1,0:T(8,128)(2,1)S(1)}, bf16[1024,512]{1,0:T(8,128)(2,1)}, u32[]{:S(2)}, u32[]{:S(2)}) collective-permute-start(bf16[1024,512]{1,0:T(8,128)(2,1)S(1)} %collective-permute-done.3.refs_6_), channel_id=1, source_target_pairs={{0,4},{4,0},{8,12},{12,8},{16,20},{20,16},{24,28},{28,24},{1,5},{5... | collective-permute-start | bytes 3145736 | tf_op jit(solution)/shard_map/ppermute | solution.py:513
  84.2 34.7 %collective-permute-start.26 = (bf16[4,128,1024]{2,1,0:T(8,128)(2,1)}, bf16[4,128,1024]{2,1,0:T(8,128)(2,1)S(1)}, u32[]{:S(2)}, u32[]{:S(2)}) collective-permute-start(bf16[4,128,1024]{2,1,0:T(8,128)(2,1)} %get-tuple-element.73), channel_id=1, source_target_pairs={{0,4},{4,0},{8,12},{12,8},{16,20},{20,16},{24,28},{28,24},{1,5},{5... | collective-permute-start | bytes 3145736 | tf_op jit(solution)/shard_map/ppermute | solution.py:513
  93.4 47.5 %collective-permute-start.33 = (bf16[4,128,1024]{2,1,0:T(8,128)(2,1)}, bf16[4,128,1024]{2,1,0:T(8,128)(2,1)}, u32[]{:S(2)}, u32[]{:S(2)}) collective-permute-start(bf16[4,128,1024]{2,1,0:T(8,128)(2,1)} %get-tuple-element.80), channel_id=1, source_target_pairs={{0,4},{4,0},{8,12},{12,8},{16,20},{20,16},{24,28},{28,24},{1,5},{5... | collective-permute-start | bytes 3145736 | tf_op jit(solution)/shard_map/ppermute | solution.py:513
  103.4 19.3 %collective-permute-start.22 = (bf16[128,1024]{1,0:T(8,128)(2,1)}, bf16[128,1024]{1,0:T(8,128)(2,1)S(1)}, u32[]{:S(2)}, u32[]{:S(2)}) collective-permute-start(bf16[128,1024]{1,0:T(8,128)(2,1)} %get-tuple-element.69), channel_id=1, source_target_pairs={{0,24},{4,28},{8,16},{12,20},{16,8},{20,12},{24,0},{28,4},{1,25},{... | collective-permute-start | bytes 786440 | tf_op jit(solution)/shard_map/ppermute | solution.py:513
  104.8 22.0 %collective-permute-start.21 = (bf16[128,1024]{1,0:T(8,128)(2,1)}, bf16[128,1024]{1,0:T(8,128)(2,1)S(1)}, u32[]{:S(2)}, u32[]{:S(2)}) collective-permute-start(bf16[128,1024]{1,0:T(8,128)(2,1)} %get-tuple-element.68), channel_id=1, source_target_pairs={{0,16},{4,20},{8,24},{12,28},{16,0},{20,4},{24,8},{28,12},{1,17},{... | collective-permute-start | bytes 786440 | tf_op jit(solution)/shard_map/ppermute | solution.py:513
  106.3 21.5 %collective-permute-start.20 = (bf16[128,1024]{1,0:T(8,128)(2,1)}, bf16[128,1024]{1,0:T(8,128)(2,1)S(1)}, u32[]{:S(2)}, u32[]{:S(2)}) collective-permute-start(bf16[128,1024]{1,0:T(8,128)(2,1)} %get-tuple-element.67), channel_id=1, source_target_pairs={{0,8},{4,12},{8,0},{12,4},{16,24},{20,28},{24,16},{28,20},{1,9},{5... | collective-permute-start | bytes 786440 | tf_op jit(solution)/shard_map/ppermute | solution.py:513
  118.9 42.6 %collective-permute-start.16 = (bf16[3,128,1024]{2,1,0:T(8,128)(2,1)}, bf16[3,128,1024]{2,1,0:T(8,128)(2,1)S(1)}, u32[]{:S(2)}, u32[]{:S(2)}) collective-permute-start(bf16[3,128,1024]{2,1,0:T(8,128)(2,1)} %get-tuple-element.64), channel_id=1, source_target_pairs={{0,1},{3,2},{4,5},{7,6},{8,9},{11,10},{12,13},{15,14},{16,17},{19,... | collective-permute-start | bytes 2359304 | tf_op jit(solution)/shard_map/ppermute | solution.py:517
  125.8 17.3 %collective-permute-start.29 = (bf16[128,1024]{1,0:T(8,128)(2,1)}, bf16[128,1024]{1,0:T(8,128)(2,1)S(1)}, u32[]{:S(2)}, u32[]{:S(2)}) collective-permute-start(bf16[128,1024]{1,0:T(8,128)(2,1)} %get-tuple-element.76), channel_id=1, source_target_pairs={{0,24},{4,28},{8,16},{12,20},{16,8},{20,12},{24,0},{28,4},{1,25},{... | collective-permute-start | bytes 786440 | tf_op jit(solution)/shard_map/ppermute | solution.py:513
  126.8 20.6 %collective-permute-start.27 = (bf16[128,1024]{1,0:T(8,128)(2,1)}, bf16[128,1024]{1,0:T(8,128)(2,1)S(1)}, u32[]{:S(2)}, u32[]{:S(2)}) collective-permute-start(bf16[128,1024]{1,0:T(8,128)(2,1)} %get-tuple-element.74), channel_id=1, source_target_pairs={{0,8},{4,12},{8,0},{12,4},{16,24},{20,28},{24,16},{28,20},{1,9},{5... | collective-permute-start | bytes 786440 | tf_op jit(solution)/shard_map/ppermute | solution.py:513
  127.8 20.3 %collective-permute-start.28 = (bf16[128,1024]{1,0:T(8,128)(2,1)}, bf16[128,1024]{1,0:T(8,128)(2,1)S(1)}, u32[]{:S(2)}, u32[]{:S(2)}) collective-permute-start(bf16[128,1024]{1,0:T(8,128)(2,1)} %get-tuple-element.75), channel_id=1, source_target_pairs={{0,16},{4,20},{8,24},{12,28},{16,0},{20,4},{24,8},{28,12},{1,17},{... | collective-permute-start | bytes 786440 | tf_op jit(solution)/shard_map/ppermute | solution.py:513
  140.9 39.3 %collective-permute-start.23 = (bf16[3,128,1024]{2,1,0:T(8,128)(2,1)}, bf16[3,128,1024]{2,1,0:T(8,128)(2,1)}, u32[]{:S(2)}, u32[]{:S(2)}) collective-permute-start(bf16[3,128,1024]{2,1,0:T(8,128)(2,1)} %get-tuple-element.71), channel_id=1, source_target_pairs={{0,1},{3,2},{4,5},{7,6},{8,9},{11,10},{12,13},{15,14},{16,17},{19,... | collective-permute-start | bytes 2359304 | tf_op jit(solution)/shard_map/ppermute | solution.py:517
  146.4 16.6 %collective-permute-start.34 = (bf16[128,1024]{1,0:T(8,128)(2,1)}, bf16[128,1024]{1,0:T(8,128)(2,1)S(1)}, u32[]{:S(2)}, u32[]{:S(2)}) collective-permute-start(bf16[128,1024]{1,0:T(8,128)(2,1)} %get-tuple-element.81), channel_id=1, source_target_pairs={{0,8},{4,12},{8,0},{12,4},{16,24},{20,28},{24,16},{28,20},{1,9},{5... | collective-permute-start | bytes 786440 | tf_op jit(solution)/shard_map/ppermute | solution.py:513
  147.4 17.0 %collective-permute-start.35 = (bf16[128,1024]{1,0:T(8,128)(2,1)}, bf16[128,1024]{1,0:T(8,128)(2,1)S(1)}, u32[]{:S(2)}, u32[]{:S(2)}) collective-permute-start(bf16[128,1024]{1,0:T(8,128)(2,1)} %get-tuple-element.82), channel_id=1, source_target_pairs={{0,16},{4,20},{8,24},{12,28},{16,0},{20,4},{24,8},{28,12},{1,17},{... | collective-permute-start | bytes 786440 | tf_op jit(solution)/shard_map/ppermute | solution.py:513
  161.5 25.0 %collective-permute-start.30 = (bf16[3,128,1024]{2,1,0:T(8,128)(2,1)}, bf16[3,128,1024]{2,1,0:T(8,128)(2,1)S(1)}, u32[]{:S(2)}, u32[]{:S(2)}) collective-permute-start(bf16[3,128,1024]{2,1,0:T(8,128)(2,1)} %get-tuple-element.78), channel_id=1, source_target_pairs={{0,1},{3,2},{4,5},{7,6},{8,9},{11,10},{12,13},{15,14},{16,17},{19,... | collective-permute-start | bytes 2359304 | tf_op jit(solution)/shard_map/ppermute | solution.py:517
  163.0 20.6 %collective-permute-start.17 = (bf16[2,128,1024]{2,1,0:T(8,128)(2,1)S(1)}, bf16[2,128,1024]{2,1,0:T(8,128)(2,1)}, u32[]{:S(2)}, u32[]{:S(2)}) collective-permute-start(bf16[2,128,1024]{2,1,0:T(8,128)(2,1)S(1)} %slice_add_fusion.3), channel_id=1, source_target_pairs={{1,2},{2,1},{5,6},{6,5},{9,10},{10,9},{13,14},{14,13},{17,18},{18,... | collective-permute-start | bytes 1572872 | tf_op jit(solution)/shard_map/ppermute | solution.py:517
  176.9 39.5 %collective-permute-start.37 = (bf16[3,128,1024]{2,1,0:T(8,128)(2,1)}, bf16[3,128,1024]{2,1,0:T(8,128)(2,1)}, u32[]{:S(2)}, u32[]{:S(2)}) collective-permute-start(bf16[3,128,1024]{2,1,0:T(8,128)(2,1)} %get-tuple-element.85), channel_id=1, source_target_pairs={{0,1},{3,2},{4,5},{7,6},{8,9},{11,10},{12,13},{15,14},{16,17},{19,... | collective-permute-start | bytes 2359304 | tf_op jit(solution)/shard_map/ppermute | solution.py:517
  182.1 32.0 %collective-permute-start.24 = (bf16[2,128,1024]{2,1,0:T(8,128)(2,1)}, bf16[2,128,1024]{2,1,0:T(8,128)(2,1)}, u32[]{:S(2)}, u32[]{:S(2)}) collective-permute-start(bf16[2,128,1024]{2,1,0:T(8,128)(2,1)} %slice_add_fusion.2), channel_id=1, source_target_pairs={{1,2},{2,1},{5,6},{6,5},{9,10},{10,9},{13,14},{14,13},{17,18},{18,... | collective-permute-start | bytes 1572872 | tf_op jit(solution)/shard_map/ppermute | solution.py:517
  185.2 33.2 %collective-permute-start.18 = (bf16[128,1024]{1,0:T(8,128)(2,1)}, bf16[128,1024]{1,0:T(8,128)(2,1)}, u32[]{:S(2)}, u32[]{:S(2)}) collective-permute-start(bf16[128,1024]{1,0:T(8,128)(2,1)} %fusion.14), channel_id=1, source_target_pairs={{1,0},{2,3},{5,4},{6,7},{9,8},{10,11},{13,12},{14,15},{17,16},{18,... | collective-permute-start | bytes 786440 | tf_op jit(solution)/shard_map/ppermute | solution.py:517
  227.1 18.5 %collective-permute-start.39 = (bf16[128,1024]{1,0:T(8,128)(2,1)S(1)}, bf16[128,1024]{1,0:T(8,128)(2,1)S(1)}, u32[]{:S(2)}, u32[]{:S(2)}) collective-permute-start(bf16[128,1024]{1,0:T(8,128)(2,1)S(1)} %fusion.11), channel_id=1, source_target_pairs={{1,0},{2,3},{5,4},{6,7},{9,8},{10,11},{13,12},{14,15},{17,16},{18,... | collective-permute-start | bytes 786440 | tf_op jit(solution)/shard_map/ppermute | solution.py:517
  (46 other events, 335.5 us)
